TPU v7x, 32 devices: a whole 2x2x4 slice. The times are simulated.
32 devices in a mesh: seq: 8 (over z, y), head: 4 (over x, core).
Axes of the slice: x: 2, y: 2, z: 4, core: 2. Of those that a mesh axis runs over, the one named last changes fastest.
Arguments:
- queries: bfloat16 [4096, 8192], P('seq', 'head'), may hold values from -6 to 6
- keys: bfloat16 [4096, 8192], P('seq', 'head'), may hold values from -6 to 6
- values: bfloat16 [4096, 8192], P('seq', 'head'), may hold values from -120 to 120
- gate: bfloat16 [4096, 8192], P('seq', 'head'), may hold values from -6 to 6
- grad_out: bfloat16 [4096, 8192], P('seq', 'head'), may hold values from -6 to 6
- gain: float32 [8192], P('head'), may hold values from 0.25 to 1.75
- tile_mask: int32 [32, 4], P('seq'), may hold values from 0 to 1, as said below
Outputs:
- grad_queries: bfloat16 [4096, 8192], P('seq', 'head')
- grad_keys: bfloat16 [4096, 8192], P('seq', 'head')
- grad_values: bfloat16 [4096, 8192], P('seq', 'head')
- grad_gate: bfloat16 [4096, 8192], P('seq', 'head')
- grad_gain: float32 [8192], P('head')
Inputs may be any that keep to these rules, and one draw needn't show every extreme that they name: `tile_mask`: entries are 0 or 1; in every slab's 4 x 4 block the diagonal is 1 and entries above it are 0.
All inputs are finite; a program needn't handle non-finite values.
Results may differ from a plain program's by a relative error of at most 0.0058.
Values sent between devices are 32-bit elements; how exact they have to be, the bound alone decides.
No kernel may reach another device: no remote copies, remote signals or barrier semaphores. Data moves between devices by JAX's collectives and lax.ppermute only.
A program may use at most 128 MiB of HBM per device.

v0:
```python
import functools

import jax
import jax.numpy as jnp
from jax import lax
from jax.experimental import pallas as pl
from jax.experimental.pallas import tpu as pltpu
from jax.sharding import PartitionSpec as P

HD = 128
EPS = 1e-06
F32 = jnp.float32
BF16 = jnp.bfloat16
HIGH = lax.Precision.HIGHEST
VMEM_LIMIT = 12 * 1024 * 1024
VMEM = pl.BlockSpec(memory_space=pltpu.VMEM)
SMEM = pl.BlockSpec(memory_space=pltpu.SMEM)
HBM = pl.BlockSpec(memory_space=pltpu.HBM)
ANY = pl.BlockSpec(memory_space=pl.ANY)
INTRA_SHARE = [1, 0, 2, 0, 1]
BACK_SHARE = [2, 2, 2, 0, 2]
BACK_SIZE = 1
LONG = 1 << 26


def dot(a, b, ca, cb, precision=None):
    return lax.dot_general(
        a, b, (((ca,), (cb,)), ((), ())), precision=precision, preferred_element_type=F32
    )


def shape(dims, dtype=F32):
    return jax.ShapeDtypeStruct(dims, dtype)


def call(kernel, name, ins, outs, scratch=(), after=(), aliases=None, cost=1):
    after = list(after)

    def run(*refs):
        kernel(*refs[: len(ins)], *refs[len(ins) + len(after) :])

    return pl.pallas_call(
        run,
        name=name,
        out_shape=[o for o, _ in outs],
        in_specs=[s for _, s in ins] + [ANY] * len(after),
        out_specs=[s for _, s in outs],
        scratch_shapes=list(scratch),
        input_output_aliases=aliases or {},
        cost_estimate=pl.CostEstimate(flops=cost, bytes_accessed=cost, transcendentals=0),
        compiler_params=pltpu.CompilerParams(vmem_limit_bytes=VMEM_LIMIT),
    )(*[pltpu.with_memory_space_constraint(a, pltpu.HBM) if s is HBM else a for a, s in ins], *after)


def part(i, size):
    return slice(i * size, (i + 1) * size)


def shard_cols(chunk, quad, d, sw):
    member = lax.rem(lax.axis_index("seq"), quad)
    return pl.ds(pl.multiple_of((chunk * quad + (member ^ d)) * sw, sw), sw)


def sum_parts(parts):
    return functools.reduce(jnp.add, parts)


def head_at(chunk, quad, d, hs, h):
    member = lax.rem(lax.axis_index("seq"), quad)
    return pl.ds(pl.multiple_of(((chunk * quad + (member ^ d)) * hs + h) * HD, HD), HD)


def start_fetch(chunk, quad, base, steps, sw, pairs, sems):
    groups = []
    for d in range(steps):
        cols = shard_cols(chunk, quad, base + d, sw)
        group = [
            pltpu.make_async_copy(src.at[:, cols], dst.at[:, part(d, sw)], sems.at[i, d])
            for i, (src, dst) in enumerate(pairs)
        ]
        for copy in group:
            copy.start()
        groups.append(group)
    return groups


def write_masks(tiles, tile, mask, keep, keep_t):
    row = lax.broadcasted_iota(jnp.int32, (tile, tile), 0)
    col = lax.broadcasted_iota(jnp.int32, (tile, tile), 1)
    for i in range(tiles):
        for j in range(tiles):
            read = mask[i, j] == 1
            if i == j:
                keep[part(i, tile), part(j, tile)] = jnp.where(read & (row >= col), 1.0, 0.0).astype(BF16)
                keep_t[part(j, tile), part(i, tile)] = jnp.where(read & (row <= col), 1.0, 0.0).astype(BF16)
            else:
                value = jnp.where(read & (row >= 0), 1.0, 0.0).astype(BF16)
                keep[part(i, tile), part(j, tile)] = value
                keep_t[part(j, tile), part(i, tile)] = value


def states_kernel(quad, hs, chunk, tiles, tile, *refs):
    sw = hs * HD
    first = chunk == 0
    srcs, refs = refs[:2], refs[2:]
    if first:
        mask, refs = refs[0], refs[1:]
    (k_out, v_out), outs, refs = refs[:2], refs[2 : 2 + quad], refs[2 + quad :]
    if first:
        (keep, keep_t), refs = refs[:2], refs[2:]
    groups = start_fetch(chunk, quad, 0, quad, sw, list(zip(srcs, (k_out, v_out))), refs[0])
    if first:
        held, mask_sem = refs[-2:]
        copy = pltpu.make_async_copy(mask, held, mask_sem.at[0])
        copy.start()
        copy.wait()
        write_masks(tiles, tile, held, keep, keep_t)
    for d in range(quad):
        for copy in groups[d]:
            copy.wait()
        write_states(outs[d], k_out[:, part(d, sw)], v_out[:, part(d, sw)], hs)


def write_states(out, a, b, hs):
    if hs == 2:
        both = dot(a, b, 0, 0)
        for h in range(hs):
            out[part(h, HD), :] = both[part(h, HD), part(h, HD)]
    else:
        for h in range(hs):
            out[part(h, HD), :] = dot(a[:, part(h, HD)], b[:, part(h, HD)], 0, 0)


def intra_kernel(quad, hs, chunk, base, steps, blk, k, v, keep, q, gate, up, gain, intra, weight):
    rows = keep.shape[0]
    for d in range(steps):
        for h in range(hs):
            mine = part(d * hs + h, HD)
            cols = part((base + d) * hs + h, HD)
            at = head_at(chunk, quad, base + d, hs, h)
            outs = []
            for j in range(rows // blk):
                ks, after = part(j, blk), slice(j * blk, rows)
                probs = dot(q[after, at], k[ks, cols], 1, 1).astype(BF16) * keep[after, ks]
                outs.append(dot(probs, v[ks, cols], 1, 0))
            for i in range(rows // blk):
                intra[part(i, blk), mine] = sum_parts([outs[j][part(i - j, blk)] for j in range(i + 1)])
            sig = jax.nn.sigmoid(gate[:, at].astype(F32))
            weight[:, mine] = up[:, at].astype(F32) * sig * gain[:, at]


def packed_rows(j, blk):
    at = j * (j + 1) // 2 * blk
    return slice(at, at + (j + 1) * blk)


def probs_kernel(hs, quad, chunk, base, steps, blk, k, q, keep_t, probs):
    for d in range(steps):
        for h in range(hs):
            cols = part((base + d) * hs + h, HD)
            at = head_at(chunk, quad, base + d, hs, h)
            for j in range(keep_t.shape[0] // blk):
                qs, end = part(j, blk), (j + 1) * blk
                one = dot(k[:end, cols], q[qs, at], 1, 1).astype(BF16) * keep_t[:end, qs]
                probs[d * hs + h, packed_rows(j, blk), :] = one


def sums_kernel(hs, chunk, first, sides, pieces_n, q, *refs):
    intras, weights = refs[:sides], refs[sides : 2 * sides]
    pieces = refs[2 * sides : 2 * sides + pieces_n]
    rest = refs[2 * sides + pieces_n :]
    before, out, attn_out = (None, *rest) if first else rest
    steps = pieces_n // sides
    squares = cross = None
    for d in range(pieces_n):
        side, at = d // steps, d % steps
        for h in range(hs):
            cols = part(at * hs + h, HD)
            prefix = pieces[d][part(h, HD), :].astype(BF16)
            attn = intras[side][:, cols] + dot(q[:, head_at(chunk, pieces_n, d, hs, h)], prefix, 1, 0)
            attn_out[:, part(d * hs + h, HD)] = attn
            wide = weights[side][:, cols]
            squares = attn * attn if squares is None else squares + attn * attn
            cross = attn * wide if cross is None else cross + attn * wide
    place = lax.broadcasted_iota(jnp.int32, (8, HD), 0)
    total = dot((place == 0).astype(F32), squares, 1, 1, HIGH)
    total = total + dot((place == 1).astype(F32), cross, 1, 1, HIGH)
    out[...] = total if first else total + before[...]


def adjoint_kernel(hs, chunk, full, sides, quad, parts_n, carried, last, queries, attns, *refs):
    weights, refs = refs[:sides], refs[sides:]
    parts, refs = refs[:parts_n], refs[parts_n:]
    gains_before, refs = refs[:carried], refs[carried:]
    da, inverse = refs[:2]
    outs = refs[2 : 2 + quad]
    factor = refs[-1]
    total = parts[0][...]
    for one in parts[1:]:
        total = total + one[...]
    place = lax.broadcasted_iota(jnp.int32, (8, HD), 0)
    mean = dot(total, (place == 0).astype(F32), 0, 0, HIGH) * (1.0 / full) + EPS
    inverse[...] = lax.rsqrt(mean)
    factor[...] = dot(total, (place == 1).astype(F32), 0, 0, HIGH) * (1.0 / full) / mean
    steps = quad // sides
    sw = hs * HD
    for d in range(quad):
        side, at = d // steps, d % steps
        rows_out = []
        for h in range(hs):
            mine = part(d * hs + h, HD)
            attn = attns[:, mine]
            wide = weights[side][:, part(at * hs + h, HD)]
            scale = inverse[...]
            da[:, mine] = ((wide - attn * factor[...]) * scale).astype(BF16)
            rows_out.append(jnp.sum(wide * attn * scale, 0, keepdims=True))
        write_states(outs[d], queries[:, shard_cols(chunk, quad, d, sw)], da[:, part(d, sw)], hs)
        if last:
            older = [g[part(d, hs), :] for g in gains_before]
            pad = outs[d].shape[0] - sw - (len(older) + 1) * hs
            zero = [jnp.zeros((pad, HD), F32)] if pad else []
            outs[d][sw:, :] = jnp.concatenate(older + rows_out + zero, 0)
        else:
            refs[2 + quad][part(d, hs), :] = jnp.concatenate(rows_out, 0)


def total_kernel(sw, pieces_n, whole, *refs):
    total = refs[0][...]
    for one in refs[1:pieces_n]:
        total = total + one[...]
    refs[pieces_n][...] = total if whole else total[:sw]
    if len(refs) > pieces_n + 1:
        refs[pieces_n + 1][...] = total[sw:]


def give_kernel(sw, quad, later, smalls_n, gate_group, *refs):
    pieces, start, smalls, outs = refs[:quad], refs[quad], refs[quad + 1 : quad + 1 + smalls_n], refs[quad + 1 + smalls_n :]
    member = lax.rem(lax.axis_index("seq"), quad)
    values = [piece[:sw, :] for piece in pieces]
    begin = start[:sw, :]
    if gate_group is not None:
        begin = begin * jnp.where(lax.axis_index("seq") // quad == gate_group, 1.0, 0.0)
    for d in range(quad):
        total = begin
        for e in range(quad):
            if e != d:
                source, target = member ^ e, member ^ d
                take = source > target if later else source < target
                total = total + values[e] * jnp.where(take, 1.0, 0.0)
        outs[d][:sw, :] = total
    if smalls_n:
        small = outs[0].shape[0] - sw
        total = smalls[0][-small:, :]
        for one in smalls[1:]:
            total = total + one[...]
        if gate_group is not None:
            total = total + start[sw:, :]
        for d in range(quad):
            outs[d][sw:, :] = total


def back_kernel(hs, quad, chunk, base, at_side, steps, blk, k, v, da, keep, keep_t, q, gate, attns, weight, inverse, probs, *rest):
    pieces, (gq, ggate, gk, gv) = rest[:steps], rest[steps:]
    rows = keep.shape[0]
    n = rows // blk
    for d in range(steps):
        for h in range(hs):
            mine = part(d * hs + h, HD)
            cols = part((base + d) * hs + h, HD)
            at = head_at(chunk, quad, base + d, hs, h)
            in_side = (at_side + d) * hs + h
            prefix = pieces[d][part(h, HD), :].astype(BF16)
            linear = dot(da[:, cols], prefix, 1, 1)
            dprobs = [
                dot(da[j * blk :, cols], v[part(j, blk), cols], 1, 1).astype(BF16) * keep[j * blk :, part(j, blk)]
                for j in range(n)
            ]
            outs = [dot(dprobs[j], k[part(j, blk), cols], 1, 0) for j in range(n)]
            for i in range(n):
                pieces_q = [linear[part(i, blk)]] + [outs[j][part(i - j, blk)] for j in range(i + 1)]
                gq[part(i, blk), mine] = sum_parts(pieces_q).astype(BF16)
            outs_v, outs_k = [], []
            for j in range(n):
                qs, end = part(j, blk), (j + 1) * blk
                outs_v.append(dot(probs[in_side, packed_rows(j, blk), :], da[qs, cols], 1, 0))
                back = dot(v[:end, cols], da[qs, cols], 1, 1).astype(BF16) * keep_t[:end, qs]
                outs_k.append(dot(back, q[qs, at], 1, 0))
            for i in range(n):
                gv[part(i, blk), mine] = sum_parts([outs_v[j][part(i, blk)] for j in range(i, n)])
                gk[part(i, blk), mine] = sum_parts([outs_k[j][part(i, blk)] for j in range(i, n)])
            sig = jax.nn.sigmoid(gate[:, at].astype(F32))
            ggate[:, mine] = (weight[:, part(in_side, HD)] * attns[:, cols] * inverse[...] * (1.0 - sig)).astype(BF16)


def finish_kernel(hs, quad, chunk, chunks, sizes, olds, last, k, v, *rest):
    n = len(sizes)
    sw = hs * HD
    (gq_parts, ggate_parts, gk_parts, gv_parts), rest = [rest[i * n : (i + 1) * n] for i in range(4)], rest[4 * n :]
    pieces, rest = rest[:quad], rest[quad:]
    if last:
        gain, rest = rest[0], rest[1:]
    rest = rest[olds:]
    gq, ggate, gk, gv, rest = *rest[:4], rest[4:]
    if last:
        ggain, rest = rest[0], rest[1:]
    gk_out, gv_out, sems = rest
    copies = []
    where = [(i, at) for i, size in enumerate(sizes) for at in range(size)]

    def store(d, i, src, dst):
        copy = pltpu.make_async_copy(src, dst.at[:, shard_cols(chunk, quad, d, sw)], sems.at[i, d])
        copy.start()
        copies.append(copy)

    for d in range(quad):
        i, at = where[d]
        store(d, 0, gq_parts[i].at[:, part(at, sw)], gq)
        store(d, 1, ggate_parts[i].at[:, part(at, sw)], ggate)
    for d in range(quad):
        i, at = where[d]
        for h in range(hs):
            mine, cols = part(at * hs + h, HD), part(d * hs + h, HD)
            suffix = pieces[d][part(h, HD), :].astype(BF16)
            gk_out[:, cols] = (gk_parts[i][:, mine] + dot(v[:, cols], suffix, 1, 1)).astype(BF16)
            gv_out[:, cols] = (gv_parts[i][:, mine] + dot(k[:, cols], suffix, 1, 0)).astype(BF16)
        store(d, 2, gk_out.at[:, part(d, sw)], gk)
        store(d, 3, gv_out.at[:, part(d, sw)], gv)
    if last:
        for c in range(chunks):
            for d in range(quad):
                for h in range(hs):
                    at = head_at(c, quad, d, hs, h)
                    row = sw + c * hs + h
                    ggain[:, at] = pieces[d][row : row + 1, :] / gain[:, at]
    for copy in copies:
        copy.wait()


def scatter(pieces, count):
    return [pieces[0]] + [
        lax.ppermute(pieces[d], "seq", [(b, b ^ d) for b in range(count)]) for d in range(1, len(pieces))
    ]


def carry(total, count, quad, later):
    groups = count // quad

    def shift(value, by):
        pairs = [(b, b + by * quad) for b in range(count - by * quad)]
        if later:
            pairs = [(t, s) for s, t in pairs]
        return lax.ppermute(value, "seq", pairs)

    if groups == 1:
        return jnp.zeros_like(total)
    total = shift(total, 1)
    by = 1
    while by < groups - 1:
        total = total + shift(total, by)
        by *= 2
    return total


def body(queries, keys, values, gate, grad_out, gain, tile_mask):
    rows, width = queries.shape
    heads = width // HD
    tiles = tile_mask.shape[0]
    tile = rows // tiles
    blk = 2 * tile if tiles % 2 == 0 else tile
    count, head_n = lax.axis_size("seq"), lax.axis_size("head")
    quad = next(g for g in (4, 2, 1) if count % g == 0 and heads % g == 0)
    chunks = 2 if heads % (2 * quad) == 0 else 1
    hs = heads // (quad * chunks)
    sw = hs * HD
    cw = quad * sw
    sides = 2 if quad % 2 == 0 else 1
    steps = quad // sides
    pw = steps * sw
    pad = -(-chunks * hs // 8) * 8
    every = range(chunks)
    final = chunks - 1
    gain_row = gain.reshape(1, width)
    full = float(width * head_n)
    dma = pltpu.SemaphoreType.DMA
    packed = (rows // blk) * (rows // blk + 1) // 2 * blk

    places = [(c, side) for c in every for side in range(sides)]

    def states(c, after):
        first = c == 0
        scratch = [dma((2, quad))]
        scratch += [pltpu.SMEM((tiles, tiles), jnp.int32), dma((1,))] if first else []
        return call(
            functools.partial(states_kernel, quad, hs, c, tiles, tile), "states",
            [(keys, HBM), (values, HBM)] + ([(tile_mask, HBM)] if first else []),
            [(shape((rows, cw), BF16), VMEM)] * 2 + [(shape((sw, HD)), VMEM)] * quad
            + ([(shape((rows, rows), BF16), VMEM)] * 2 if first else []),
            scratch, after,
        )

    def intra(c, side, k, v, after):
        return call(
            functools.partial(intra_kernel, quad, hs, c, side * steps, steps, blk), "intra",
            [(k, VMEM), (v, VMEM), (keep, VMEM), (queries, VMEM), (gate, VMEM), (grad_out, VMEM), (gain_row, VMEM)],
            [(shape((rows, pw)), VMEM)] * 2, [], after,
        )

    def token_sums(c, lots, prefix, before, after):
        extra = [] if before is None else [(before, VMEM)]
        return call(
            functools.partial(sums_kernel, hs, c, before is None, sides, quad), "token_sums",
            [(queries, VMEM)] + [(lot[i], VMEM) for i in (0, 1) for lot in lots] + [(p, VMEM) for p in prefix] + extra,
            [(shape((8, rows)), VMEM), (shape((rows, cw)), VMEM)], (), after, cost=LONG,
        )

    def adjoints(c, attn, parts, gains, after):
        last = c == final
        outs = [(shape((rows, cw), BF16), VMEM), (shape((rows, HD)), VMEM)]
        outs += [(shape((sw + (pad if last else 0), HD)), VMEM)] * quad
        if not last:
            outs += [(shape((quad * hs, HD)), VMEM)]
        return call(
            functools.partial(adjoint_kernel, hs, c, full, sides, quad, head_n, len(gains), last), "adjoints",
            [(queries, VMEM), (attn, VMEM)] + [(lot[1], VMEM) for lot in lots[c]] + [(p, VMEM) for p in parts]
            + [(g, VMEM) for g in gains],
            outs, [pltpu.VMEM((rows, HD), F32)], after,
        )

    def probabilities(c, side, k, after):
        return call(
            functools.partial(probs_kernel, hs, quad, c, side * steps, steps, blk), "probs",
            [(k, VMEM), (queries, VMEM), (keep_t, VMEM)], [(shape((steps * hs, packed, blk), BF16), VMEM)], [], after,
        )[0]

    def totals(pieces, whole, after):
        size = pieces[0].shape[0]
        small = 0 if whole else size - sw
        return call(
            functools.partial(total_kernel, sw, quad, whole), "total", [(p, VMEM) for p in pieces],
            [(shape((size if whole else sw, HD)), VMEM)] + ([(shape((small, HD)), VMEM)] if small else []), (), after,
        )

    def give(pieces, start, smalls, later, gate_group, after):
        size = pieces[0].shape[0]
        return call(
            functools.partial(give_kernel, sw, quad, later, len(smalls), gate_group), "give",
            [(p, VMEM) for p in pieces] + [(start, VMEM)] + [(s, VMEM) for s in smalls],
            [(shape((size, HD)), VMEM)] * quad, (), after,
        )

    def back(c, base, size, k, v, da, inverse, prefix, after):
        side = base // steps
        ins = [(k, VMEM), (v, VMEM), (da, VMEM), (keep, VMEM), (keep_t, VMEM), (queries, VMEM), (gate, VMEM)]
        ins += [(attns[c], VMEM), (lots[c][side][1], VMEM), (inverse, VMEM), (probs[(c, side)], VMEM)]
        ins += [(p, VMEM) for p in prefix[base : base + size]]
        return call(
            functools.partial(back_kernel, hs, quad, c, base, base % steps, size, blk), "back", ins,
            [(shape((rows, size * sw), BF16), VMEM)] * 2 + [(shape((rows, size * sw)), VMEM)] * 2, [], after,
        )

    def finish(c, k, v, suffix, outs, after):
        last = c == final
        parts = halves[c]
        ins = [(k, VMEM), (v, VMEM)] + [(p[i], VMEM) for i in range(4) for p in parts] + [(s, VMEM) for s in suffix]
        ins += [(gain_row, VMEM)] if last else []
        aliases = {len(ins) + i: i for i in range(len(outs))}
        sizes = tuple(p[0].shape[1] // sw for p in parts)
        return call(
            functools.partial(finish_kernel, hs, quad, c, chunks, sizes, len(outs), last), "finish",
            ins + [(o, HBM) for o in outs],
            [(shape((rows, width), BF16), HBM)] * 4 + ([(shape((1, width)), VMEM)] if last else []),
            [pltpu.VMEM((rows, cw), BF16)] * 2 + [dma((4, quad))], after, aliases, cost=LONG,
        )

    def scan(messages, later, jobs):
        met = [scatter(m, count) for m in messages]
        done = messages[-1][:1]
        starts, smalls, gates = [], [[] for _ in every], [None for _ in every]
        pair = count == 2 * quad
        for c in every:
            done = jobs(c, done)
            total, *small = totals(met[c], pair, done)
            done = [total]
            if pair:
                starts.append(lax.ppermute(total, "seq", [(b, b ^ quad) for b in range(count)]))
                smalls[c] = [total] if total.shape[0] > sw else []
                gates[c] = 0 if later else 1
                continue
            starts.append(carry(total, count, quad, later))
            if small:
                smalls[c] = small + [
                    lax.ppermute(small[0], "seq", [(b, (b + s * quad) % count) for b in range(count)])
                    for s in range(1, count // quad)
                ]
        gives = []
        for c in every:
            done = jobs(chunks + c, done)
            out = give(met[c], starts[c], smalls[c], later, gates[c], done)
            done = out[:1]
            gives.append(scatter(out, count))
        return gives, jobs(2 * chunks, done)

    kv, messages, after = [], [], []
    for c in every:
        k, v, *pieces = states(c, after)
        if c == 0:
            keep, keep_t = pieces[quad : quad + 2]
        pieces = pieces[:quad]
        after = pieces[:1]
        kv.append((k, v))
        messages.append(pieces)
    lots = [[None] * sides for _ in every]
    def lots_of(items, share):
        cuts, total = [], 0
        for one in share:
            total += one
            cuts.append(round(total * len(items) / sum(share)))
        return [items[i:j] for i, j in zip([0] + cuts, cuts)]

    def windows(share):
        if chunks == 2:
            return share
        return [share[0] + share[1], share[2] + share[3], share[4]]

    intra_lots = lots_of(places, windows(INTRA_SHARE))

    def intra_jobs(window, after):
        for c, side in intra_lots[window]:
            lots[c][side] = intra(c, side, *kv[c], after)
            after = lots[c][side][:1]
        return after

    prefix, after = scan(messages, False, intra_jobs)
    sums, attns = None, []
    for c in every:
        sums, attn = token_sums(c, lots[c], prefix[c], sums, after)
        attns.append(attn)
        after = []
    parts = [sums] + [lax.ppermute(sums, "head", [(b, b ^ d) for b in range(head_n)]) for d in range(1, head_n)]
    after, probs = [sums], {}
    for place in places:
        probs[place] = probabilities(*place, kv[place[0]][0], after)
        after = [probs[place]]

    das, messages, gains = [], [], []
    for c in every:
        da, inverse, *pieces = adjoints(c, attns[c], parts, gains if c == final else [], after)
        after = []
        das.append(da)
        messages.append(pieces[:quad])
        gains += pieces[quad:]
    halves = [[] for _ in every]
    size = min(BACK_SIZE, steps)
    back_lots = lots_of([(c, d) for c in every for d in range(0, quad, size)], windows(BACK_SHARE))

    def back_jobs(window, after):
        for c, d in back_lots[window]:
            halves[c].append(back(c, d, size, *kv[c], das[c], inverse, prefix[c], after))
            after = halves[c][-1][2:3]
        return after

    suffix, after = scan(messages, True, back_jobs)
    outs = []
    for c in every:
        outs = finish(c, *kv[c], suffix[c], outs[:4], after)
        after = []
    gq, ggate, gk, gv, ggain = outs
    return gq, gk, gv, ggate, ggain.reshape(width)


def solution(mesh):
    spec = P("seq", "head")
    return jax.shard_map(
        body, mesh=mesh, in_specs=(spec,) * 5 + (P("head"), P("seq", None)), out_specs=(spec,) * 4 + (P("head"),),
        check_vma=False,
    )
```

profile of v0, /device:TPU:0, one launch (start us, length us, event | category | flops | bytes accessed | tf_op | source)
XLA Modules:
  0.0 89.8 jit_solution(1329916886013830322)
XLA Ops:
  0.6 2.5 %states.2 = (bf16[512,1024]{1,0:T(8,128)(2,1)S(1)}, bf16[512,1024]{1,0:T(8,128)(2,1)S(1)}, f32[256,128]{1,0:T(8,128)S(1)}, f32[256,128]{1,0:T(8,128)S(1)}, f32[2...) custom-call(bf16[512,2048]{1,0:T(8,128)(2,1)} %refs_0_.7, ...), custom_call_target="tpu_custom_call" | custom-call | flops 1 | bytes 1 | tf_op jit(solution)/shard_map/states/pallas_call | solution.py:42
  3.2 3.0 %collective-permute-start.3 = (f32[256,128]{1,0:T(8,128)S(1)}, f32[256,128]{1,0:T(8,128)S(1)}, u32[]{:S(2)}, u32[]{:S(2)}) collective-permute-start(f32[256,128]{1,0:T(8,128)S(1)} %get-tuple-element.110), channel_id=1, source_target_pairs={{0,4},{4,0},{8,12},{12,8},{16,20},{20,16},{24,28},{28,24},{1,5},{5... | collective-permute-start | bytes 393224 | tf_op jit(solution)/shard_map/ppermute | solution.py:341
  7.8 2.5 %states.3 = (bf16[512,1024]{1,0:T(8,128)(2,1)S(1)}, bf16[512,1024]{1,0:T(8,128)(2,1)S(1)}, f32[256,128]{1,0:T(8,128)S(1)}, f32[256,128]{1,0:T(8,128)S(1)}, f32[2...) custom-call(bf16[512,2048]{1,0:T(8,128)(2,1)} %refs_0_.7, bf16[512,2048]{1,0:T(8,128)(2,1)} %refs_1_.7, ...), custom_call_target="tpu_custom_call" | custom-call | flops 1 | bytes 1 | tf_op jit(solution)/shard_map/states/pallas_call | solution.py:42
  10.4 2.0 %collective-permute-start = (f32[256,128]{1,0:T(8,128)S(1)}, f32[256,128]{1,0:T(8,128)S(1)}, u32[]{:S(2)}, u32[]{:S(2)}) collective-permute-start(f32[256,128]{1,0:T(8,128)S(1)} %get-tuple-element.107), channel_id=1, source_target_pairs={{0,4},{4,0},{8,12},{12,8},{16,20},{20,16},{24,28},{28,24},{1,5},{5... | collective-permute-start | bytes 393224 | tf_op jit(solution)/shard_map/ppermute | solution.py:341
  15.5 3.0 %collective-permute-start.7 = (f32[256,128]{1,0:T(8,128)S(1)}, f32[256,128]{1,0:T(8,128)S(1)}, u32[]{:S(2)}, u32[]{:S(2)}) collective-permute-start(f32[256,128]{1,0:T(8,128)S(1)} %total.4.refs_4_), channel_id=1, source_target_pairs={{0,16},{4,20},{8,24},{12,28},{16,0},{20,4},{24,8},{28,12},{1,17},{... | collective-permute-start | bytes 393224 | tf_op jit(solution)/shard_map/ppermute | solution.py:485
  21.2 2.9 %collective-permute-start.6 = (f32[256,128]{1,0:T(8,128)S(1)}, f32[256,128]{1,0:T(8,128)S(1)}, u32[]{:S(2)}, u32[]{:S(2)}) collective-permute-start(f32[256,128]{1,0:T(8,128)S(1)} %total.5.refs_7_), channel_id=1, source_target_pairs={{0,16},{4,20},{8,24},{12,28},{16,0},{20,4},{24,8},{28,12},{1,17},{... | collective-permute-start | bytes 393224 | tf_op jit(solution)/shard_map/ppermute | solution.py:485
  28.8 1.6 %collective-permute-start.12 = (f32[256,128]{1,0:T(8,128)S(1)}, f32[256,128]{1,0:T(8,128)S(1)}, u32[]{:S(2)}, u32[]{:S(2)}) collective-permute-start(f32[256,128]{1,0:T(8,128)S(1)} %get-tuple-element.127), channel_id=1, source_target_pairs={{0,8},{4,12},{8,0},{12,4},{16,24},{20,28},{24,16},{28,20},{1,9},{5... | collective-permute-start | bytes 393224 | tf_op jit(solution)/shard_map/ppermute | solution.py:341
  42.1 1.6 %collective-permute-start.15 = (f32[8,512]{1,0:T(8,128)S(1)}, f32[8,512]{1,0:T(8,128)S(1)}, u32[]{:S(2)}, u32[]{:S(2)}) collective-permute-start(f32[8,512]{1,0:T(8,128)S(1)} %get-tuple-element.131.refs_3_.refs_4_), channel_id=1, source_target_pairs={{0,2},{1,3},{2,0},{3,1},{4,6},{5,7},{6,4},{7,5},{8,10},{9,11},{10,... | collective-permute-start | bytes 49160 | tf_op jit(solution)/shard_map/ppermute | solution.py:539
  46.7 2.4 %adjoints.2 = (bf16[512,1024]{1,0:T(8,128)(2,1)S(1)}, f32[512,128]{1,0:T(8,128)}, f32[256,128]{1,0:T(8,128)S(1)}, f32[256,128]{1,0:T(8,128)S(1)}, f32[256,128]{1...) custom-call(bf16[512,2048]{1,0:T(8,128)(2,1)S(1)} %copy-done, ...), custom_call_target="tpu_custom_call" | custom-call | flops 1 | bytes 1 | tf_op jit(solution)/shard_map/adjoints/pallas_call | solution.py:42
  52.6 1.8 %adjoints.3 = (bf16[512,1024]{1,0:T(8,128)(2,1)S(1)}, f32[512,128]{1,0:T(8,128)S(1)}, f32[264,128]{1,0:T(8,128)S(1)}, f32[264,128]{1,0:T(8,128)S(1)}, f32[264,128]{1,0:T(8,128)S(1)}, /*index=5*/f32[264,128]{1,0:T(8,128)S(1)}) custom-call(bf16[512,2048]{1,0:T(8,128)(2,1)S(1)} %copy-done, f32[512,1024]{1,0:T(8,128)S(1)} %get-tuple-element.130.refs_1_.refs_7_, ...), custom_call_target="tpu_custom_call" | custom-call | flops 1 | bytes 1 | tf_op jit(solution)/shard_map/adjoints/pallas_call | solution.py:42
  57.9 1.6 %back.8 = (bf16[512,256]{1,0:T(8,128)(2,1)S(1)}, bf16[512,256]{1,0:T(8,128)(2,1)S(1)}, f32[512,256]{1,0:T(8,128)S(1)}, f32[512,256]{1,0:T(8,128)S(1)}) custom-call(bf16[512,1024]{1,0:T(8,128)(2,1)S(1)} %get-tuple-element.104.refs_0_, bf16[512,1024]{1,0:T(8,128)(2,1)S(1)} %get-tuple-element.105.refs_1_, bf16[512,1024]{1,0:T(8,128)(2,1)S(1)} %get-tuple-element.141.refs_2_, ...), custom_call_target="tpu_custom_call" | custom-call | flops 1 | bytes 1 | tf_op jit(solution)/shard_map/back/pallas_call | solution.py:42
  59.6 1.6 %back.9 = (bf16[512,256]{1,0:T(8,128)(2,1)S(1)}, bf16[512,256]{1,0:T(8,128)(2,1)S(1)}, f32[512,256]{1,0:T(8,128)S(1)}, f32[512,256]{1,0:T(8,128)S(1)}) custom-call(bf16[512,1024]{1,0:T(8,128)(2,1)S(1)} %get-tuple-element.104.refs_0_, bf16[512,1024]{1,0:T(8,128)(2,1)S(1)} %get-tuple-element.105.refs_1_, bf16[512,1024]{1,0:T(8,128)(2,1)S(1)} %get-tuple-element.141.refs_2_, ...), custom_call_target="tpu_custom_call" | custom-call | flops 1 | bytes 1 | tf_op jit(solution)/shard_map/back/pallas_call | solution.py:42
  62.5 1.7 %back.10 = (bf16[512,256]{1,0:T(8,128)(2,1)S(1)}, bf16[512,256]{1,0:T(8,128)(2,1)S(1)}, f32[512,256]{1,0:T(8,128)S(1)}, f32[512,256]{1,0:T(8,128)S(1)}) custom-call(bf16[512,1024]{1,0:T(8,128)(2,1)S(1)} %get-tuple-element.104.refs_0_, bf16[512,1024]{1,0:T(8,128)(2,1)S(1)} %get-tuple-element.105.refs_1_, bf16[512,1024]{1,0:T(8,128)(2,1)S(1)} %get-tuple-element.141.refs_2_, ...), custom_call_target="tpu_custom_call" | custom-call | flops 1 | bytes 1 | tf_op jit(solution)/shard_map/back/pallas_call | solution.py:42
  64.1 1.6 %back.11 = (bf16[512,256]{1,0:T(8,128)(2,1)S(1)}, bf16[512,256]{1,0:T(8,128)(2,1)S(1)}, f32[512,256]{1,0:T(8,128)S(1)}, f32[512,256]{1,0:T(8,128)S(1)}) custom-call(bf16[512,1024]{1,0:T(8,128)(2,1)S(1)} %get-tuple-element.104.refs_0_, bf16[512,1024]{1,0:T(8,128)(2,1)S(1)} %get-tuple-element.105.refs_1_, bf16[512,1024]{1,0:T(8,128)(2,1)S(1)} %get-tuple-element.141.refs_2_, ...), custom_call_target="tpu_custom_call" | custom-call | flops 1 | bytes 1 | tf_op jit(solution)/shard_map/back/pallas_call | solution.py:42
  65.8 1.9 %collective-permute-start.23 = (f32[264,128]{1,0:T(8,128)S(1)}, f32[264,128]{1,0:T(8,128)S(1)}, u32[]{:S(2)}, u32[]{:S(2)}) collective-permute-start(f32[264,128]{1,0:T(8,128)S(1)} %total.7.refs_12_.refs_5_), channel_id=1, source_target_pairs={{0,16},{4,20},{8,24},{12,28},{16,0},{20,4},{24,8},{28,12},{1,17},{... | collective-permute-start | bytes 405512 | tf_op jit(solution)/shard_map/ppermute | solution.py:485
  67.7 1.9 %back.12 = (bf16[512,256]{1,0:T(8,128)(2,1)S(1)}, bf16[512,256]{1,0:T(8,128)(2,1)S(1)}, f32[512,256]{1,0:T(8,128)S(1)}, f32[512,256]{1,0:T(8,128)S(1)}) custom-call(bf16[512,1024]{1,0:T(8,128)(2,1)S(1)} %get-tuple-element.101.refs_0_, bf16[512,1024]{1,0:T(8,128)(2,1)S(1)} %get-tuple-element.102.refs_1_, bf16[512,1024]{1,0:T(8,128)(2,1)S(1)} %get-tuple-element.135.refs_2_, ...), custom_call_target="tpu_custom_call" | custom-call | flops 1 | bytes 1 | tf_op jit(solution)/shard_map/back/pallas_call | solution.py:42
  69.6 1.6 %back.13 = (bf16[512,256]{1,0:T(8,128)(2,1)S(1)}, bf16[512,256]{1,0:T(8,128)(2,1)S(1)}, f32[512,256]{1,0:T(8,128)S(1)}, f32[512,256]{1,0:T(8,128)S(1)}) custom-call(bf16[512,1024]{1,0:T(8,128)(2,1)S(1)} %get-tuple-element.101.refs_0_, bf16[512,1024]{1,0:T(8,128)(2,1)S(1)} %get-tuple-element.102.refs_1_, bf16[512,1024]{1,0:T(8,128)(2,1)S(1)} %get-tuple-element.135.refs_2_, ...), custom_call_target="tpu_custom_call" | custom-call | flops 1 | bytes 1 | tf_op jit(solution)/shard_map/back/pallas_call | solution.py:42
  71.2 2.2 %collective-permute-done.24.refs_4_ = f32[256,128]{1,0:T(8,128)S(1)} collective-permute-done((f32[256,128]{1,0:T(8,128)S(1)}, f32[256,128]{1,0:T(8,128)S(1)}, u32[]{:S(2)}, u32[]{:S(2)}) %collective-permute-start.24) | collective-permute-done | bytes 131104 | tf_op jit(solution)/shard_map/ppermute | solution.py:485
  74.0 3.1 %collective-permute-start.30 = (f32[256,128]{1,0:T(8,128)S(1)}, f32[256,128]{1,0:T(8,128)S(1)}, u32[]{:S(2)}, u32[]{:S(2)}) collective-permute-start(f32[256,128]{1,0:T(8,128)S(1)} %get-tuple-element.185), channel_id=1, source_target_pairs={{0,12},{4,8},{8,4},{12,0},{16,28},{20,24},{24,20},{28,16},{1,13},{... | collective-permute-start | bytes 393224 | tf_op jit(solution)/shard_map/ppermute | solution.py:341
  77.9 3.0 %collective-permute-done.28.refs_19_ = f32[256,128]{1,0:T(8,128)S(1)} collective-permute-done((f32[256,128]{1,0:T(8,128)S(1)}, f32[256,128]{1,0:T(8,128)S(1)}, u32[]{:S(2)}, u32[]{:S(2)}) %collective-permute-start.28) | collective-permute-done | bytes 131104 | tf_op jit(solution)/shard_map/ppermute | solution.py:341
  80.8 1.7 %back.14 = (bf16[512,256]{1,0:T(8,128)(2,1)S(1)}, bf16[512,256]{1,0:T(8,128)(2,1)S(1)}, f32[512,256]{1,0:T(8,128)S(1)}, f32[512,256]{1,0:T(8,128)S(1)}) custom-call(bf16[512,1024]{1,0:T(8,128)(2,1)S(1)} %get-tuple-element.101.refs_0_, bf16[512,1024]{1,0:T(8,128)(2,1)S(1)} %get-tuple-element.102.refs_1_, bf16[512,1024]{1,0:T(8,128)(2,1)S(1)} %get-tuple-element.135.refs_2_, ...), custom_call_target="tpu_custom_call" | custom-call | flops 1 | bytes 1 | tf_op jit(solution)/shard_map/back/pallas_call | solution.py:42
  82.5 1.6 %back.15 = (bf16[512,256]{1,0:T(8,128)(2,1)S(1)}, bf16[512,256]{1,0:T(8,128)(2,1)S(1)}, f32[512,256]{1,0:T(8,128)S(1)}, f32[512,256]{1,0:T(8,128)S(1)}) custom-call(bf16[512,1024]{1,0:T(8,128)(2,1)S(1)} %get-tuple-element.101.refs_0_, bf16[512,1024]{1,0:T(8,128)(2,1)S(1)} %get-tuple-element.102.refs_1_, bf16[512,1024]{1,0:T(8,128)(2,1)S(1)} %get-tuple-element.135.refs_2_, ...), custom_call_target="tpu_custom_call" | custom-call | flops 1 | bytes 1 | tf_op jit(solution)/shard_map/back/pallas_call | solution.py:42
  84.2 2.4 %finish.2 = (bf16[512,2048]{1,0:T(8,128)(2,1)}, bf16[512,2048]{1,0:T(8,128)(2,1)}, bf16[512,2048]{1,0:T(8,128)(2,1)}, bf16[512,2048]{1,0:T(8,128)(2,1)}) custom-call(bf16[512,1024]{1,0:T(8,128)(2,1)S(1)} %get-tuple-element.104.refs_0_, bf16[512,1024]{1,0:T(8,128)(2,1)S(1)} %get-tuple-element.105.refs_1_, bf16[512,256]{1,0:T(8,128)(2,1)S(1)} %get-tuple-element.171.refs_2_, ...), custom_call_target="tpu_custom_call" | custom-call | flops 67108864 | bytes 67108864 | tf_op jit(solution)/shard_map/finish/pallas_call | solution.py:42
  86.7 2.9 %finish.3 = (bf16[512,2048]{1,0:T(8,128)(2,1)}, bf16[512,2048]{1,0:T(8,128)(2,1)}, bf16[512,2048]{1,0:T(8,128)(2,1)}, bf16[512,2048]{1,0:T(8,128)(2,1)}, f32[1,2048]{1,0:T(1,128)}) custom-call(bf16[512,1024]{1,0:T(8,128)(2,1)S(1)} %get-tuple-element.101.refs_0_, ...), custom_call_target="tpu_custom_call", output_to_operand_aliasing={{0}: (23, {}), {1}: (24, {}), {2}: (25, {}), {3}: (26, {})} | custom-call | flops 67108864 | bytes 67108864 | tf_op jit(solution)/shard_map/finish/pallas_call | solution.py:42
  (78 shorter events, 36.6 us)
Async XLA Ops:
  3.2 10.7 %collective-permute-start.3 = (f32[256,128]{1,0:T(8,128)S(1)}, f32[256,128]{1,0:T(8,128)S(1)}, u32[]{:S(2)}, u32[]{:S(2)}) collective-permute-start(f32[256,128]{1,0:T(8,128)S(1)} %get-tuple-element.110), channel_id=1, source_target_pairs={{0,4},{4,0},{8,12},{12,8},{16,20},{20,16},{24,28},{28,24},{1,5},{5... | collective-permute-start | bytes 393224 | tf_op jit(solution)/shard_map/ppermute | solution.py:341
  6.2 9.2 %collective-permute-start.4 = (f32[256,128]{1,0:T(8,128)S(1)}, f32[256,128]{1,0:T(8,128)S(1)}, u32[]{:S(2)}, u32[]{:S(2)}) collective-permute-start(f32[256,128]{1,0:T(8,128)S(1)} %get-tuple-element.111), channel_id=1, source_target_pairs={{0,8},{4,12},{8,0},{12,4},{16,24},{20,28},{24,16},{28,20},{1,9},{5... | collective-permute-start | bytes 393224 | tf_op jit(solution)/shard_map/ppermute | solution.py:341
  7.8 7.6 %collective-permute-start.5 = (f32[256,128]{1,0:T(8,128)S(1)}, f32[256,128]{1,0:T(8,128)S(1)}, u32[]{:S(2)}, u32[]{:S(2)}) collective-permute-start(f32[256,128]{1,0:T(8,128)S(1)} %get-tuple-element.112), channel_id=1, source_target_pairs={{0,12},{4,8},{8,4},{12,0},{16,28},{20,24},{24,20},{28,16},{1,13},{... | collective-permute-start | bytes 393224 | tf_op jit(solution)/shard_map/ppermute | solution.py:341
  10.4 8.2 %collective-permute-start = (f32[256,128]{1,0:T(8,128)S(1)}, f32[256,128]{1,0:T(8,128)S(1)}, u32[]{:S(2)}, u32[]{:S(2)}) collective-permute-start(f32[256,128]{1,0:T(8,128)S(1)} %get-tuple-element.107), channel_id=1, source_target_pairs={{0,4},{4,0},{8,12},{12,8},{16,20},{20,16},{24,28},{28,24},{1,5},{5... | collective-permute-start | bytes 393224 | tf_op jit(solution)/shard_map/ppermute | solution.py:341
  12.3 7.3 %collective-permute-start.1 = (f32[256,128]{1,0:T(8,128)S(1)}, f32[256,128]{1,0:T(8,128)S(1)}, u32[]{:S(2)}, u32[]{:S(2)}) collective-permute-start(f32[256,128]{1,0:T(8,128)S(1)} %get-tuple-element.108), channel_id=1, source_target_pairs={{0,8},{4,12},{8,0},{12,4},{16,24},{20,28},{24,16},{28,20},{1,9},{5... | collective-permute-start | bytes 393224 | tf_op jit(solution)/shard_map/ppermute | solution.py:341
  15.5 11.6 %collective-permute-start.7 = (f32[256,128]{1,0:T(8,128)S(1)}, f32[256,128]{1,0:T(8,128)S(1)}, u32[]{:S(2)}, u32[]{:S(2)}) collective-permute-start(f32[256,128]{1,0:T(8,128)S(1)} %total.4.refs_4_), channel_id=1, source_target_pairs={{0,16},{4,20},{8,24},{12,28},{16,0},{20,4},{24,8},{28,12},{1,17},{... | collective-permute-start | bytes 393224 | tf_op jit(solution)/shard_map/ppermute | solution.py:485
  21.2 9.6 %collective-permute-start.6 = (f32[256,128]{1,0:T(8,128)S(1)}, f32[256,128]{1,0:T(8,128)S(1)}, u32[]{:S(2)}, u32[]{:S(2)}) collective-permute-start(f32[256,128]{1,0:T(8,128)S(1)} %total.5.refs_7_), channel_id=1, source_target_pairs={{0,16},{4,20},{8,24},{12,28},{16,0},{20,4},{24,8},{28,12},{1,17},{... | collective-permute-start | bytes 393224 | tf_op jit(solution)/shard_map/ppermute | solution.py:485
  27.3 7.7 %collective-permute-start.11 = (f32[256,128]{1,0:T(8,128)S(1)}, f32[256,128]{1,0:T(8,128)S(1)}, u32[]{:S(2)}, u32[]{:S(2)}) collective-permute-start(f32[256,128]{1,0:T(8,128)S(1)} %get-tuple-element.126), channel_id=1, source_target_pairs={{0,4},{4,0},{8,12},{12,8},{16,20},{20,16},{24,28},{28,24},{1,5},{5... | collective-permute-start | bytes 393224 | tf_op jit(solution)/shard_map/ppermute | solution.py:341
  28.8 8.0 %collective-permute-start.12 = (f32[256,128]{1,0:T(8,128)S(1)}, f32[256,128]{1,0:T(8,128)S(1)}, u32[]{:S(2)}, u32[]{:S(2)}) collective-permute-start(f32[256,128]{1,0:T(8,128)S(1)} %get-tuple-element.127), channel_id=1, source_target_pairs={{0,8},{4,12},{8,0},{12,4},{16,24},{20,28},{24,16},{28,20},{1,9},{5... | collective-permute-start | bytes 393224 | tf_op jit(solution)/shard_map/ppermute | solution.py:341
  30.4 7.4 %collective-permute-start.13 = (f32[256,128]{1,0:T(8,128)S(1)}, f32[256,128]{1,0:T(8,128)S(1)}, u32[]{:S(2)}, u32[]{:S(2)}) collective-permute-start(f32[256,128]{1,0:T(8,128)S(1)} %get-tuple-element.128), channel_id=1, source_target_pairs={{0,12},{4,8},{8,4},{12,0},{16,28},{20,24},{24,20},{28,16},{1,13},{... | collective-permute-start | bytes 393224 | tf_op jit(solution)/shard_map/ppermute | solution.py:341
  31.0 8.3 %collective-permute-start.8 = (f32[256,128]{1,0:T(8,128)S(1)}, f32[256,128]{1,0:T(8,128)S(1)}, u32[]{:S(2)}, u32[]{:S(2)}) collective-permute-start(f32[256,128]{1,0:T(8,128)S(1)} %get-tuple-element.121), channel_id=1, source_target_pairs={{0,4},{4,0},{8,12},{12,8},{16,20},{20,16},{24,28},{28,24},{1,5},{5... | collective-permute-start | bytes 393224 | tf_op jit(solution)/shard_map/ppermute | solution.py:341
  49.1 7.7 %collective-permute-start.20 = (f32[256,128]{1,0:T(8,128)S(1)}, f32[256,128]{1,0:T(8,128)S(1)}, u32[]{:S(2)}, u32[]{:S(2)}) collective-permute-start(f32[256,128]{1,0:T(8,128)S(1)} %get-tuple-element.143), channel_id=1, source_target_pairs={{0,4},{4,0},{8,12},{12,8},{16,20},{20,16},{24,28},{28,24},{1,5},{5... | collective-permute-start | bytes 393224 | tf_op jit(solution)/shard_map/ppermute | solution.py:341
  50.5 10.7 %collective-permute-start.21 = (f32[256,128]{1,0:T(8,128)S(1)}, f32[256,128]{1,0:T(8,128)S(1)}, u32[]{:S(2)}, u32[]{:S(2)}) collective-permute-start(f32[256,128]{1,0:T(8,128)S(1)} %get-tuple-element.144), channel_id=1, source_target_pairs={{0,8},{4,12},{8,0},{12,4},{16,24},{20,28},{24,16},{28,20},{1,9},{5... | collective-permute-start | bytes 393224 | tf_op jit(solution)/shard_map/ppermute | solution.py:341
  51.5 9.7 %collective-permute-start.22 = (f32[256,128]{1,0:T(8,128)S(1)}, f32[256,128]{1,0:T(8,128)S(1)}, u32[]{:S(2)}, u32[]{:S(2)}) collective-permute-start(f32[256,128]{1,0:T(8,128)S(1)} %get-tuple-element.145), channel_id=1, source_target_pairs={{0,12},{4,8},{8,4},{12,0},{16,28},{20,24},{24,20},{28,16},{1,13},{... | collective-permute-start | bytes 393224 | tf_op jit(solution)/shard_map/ppermute | solution.py:341
  54.4 11.4 %collective-permute-start.17 = (f32[264,128]{1,0:T(8,128)S(1)}, f32[264,128]{1,0:T(8,128)S(1)}, u32[]{:S(2)}, u32[]{:S(2)}) collective-permute-start(f32[264,128]{1,0:T(8,128)S(1)} %get-tuple-element.138), channel_id=1, source_target_pairs={{0,4},{4,0},{8,12},{12,8},{16,20},{20,16},{24,28},{28,24},{1,5},{5... | collective-permute-start | bytes 405512 | tf_op jit(solution)/shard_map/ppermute | solution.py:341
  55.9 9.9 %collective-permute-start.18 = (f32[264,128]{1,0:T(8,128)S(1)}, f32[264,128]{1,0:T(8,128)S(1)}, u32[]{:S(2)}, u32[]{:S(2)}) collective-permute-start(f32[264,128]{1,0:T(8,128)S(1)} %get-tuple-element.139), channel_id=1, source_target_pairs={{0,8},{4,12},{8,0},{12,4},{16,24},{20,28},{24,16},{28,20},{1,9},{5... | collective-permute-start | bytes 405512 | tf_op jit(solution)/shard_map/ppermute | solution.py:341
  56.8 8.9 %collective-permute-start.19 = (f32[264,128]{1,0:T(8,128)S(1)}, f32[264,128]{1,0:T(8,128)S(1)}, u32[]{:S(2)}, u32[]{:S(2)}) collective-permute-start(f32[264,128]{1,0:T(8,128)S(1)} %get-tuple-element.140), channel_id=1, source_target_pairs={{0,12},{4,8},{8,4},{12,0},{16,28},{20,24},{24,20},{28,16},{1,13},{... | collective-permute-start | bytes 405512 | tf_op jit(solution)/shard_map/ppermute | solution.py:341
  61.3 12.1 %collective-permute-start.24 = (f32[256,128]{1,0:T(8,128)S(1)}, f32[256,128]{1,0:T(8,128)S(1)}, u32[]{:S(2)}, u32[]{:S(2)}) collective-permute-start(f32[256,128]{1,0:T(8,128)S(1)} %total.6.refs_12_), channel_id=1, source_target_pairs={{0,16},{4,20},{8,24},{12,28},{16,0},{20,4},{24,8},{28,12},{1,17},{... | collective-permute-start | bytes 393224 | tf_op jit(solution)/shard_map/ppermute | solution.py:485
  65.8 11.3 %collective-permute-start.23 = (f32[264,128]{1,0:T(8,128)S(1)}, f32[264,128]{1,0:T(8,128)S(1)}, u32[]{:S(2)}, u32[]{:S(2)}) collective-permute-start(f32[264,128]{1,0:T(8,128)S(1)} %total.7.refs_12_.refs_5_), channel_id=1, source_target_pairs={{0,16},{4,20},{8,24},{12,28},{16,0},{20,4},{24,8},{28,12},{1,17},{... | collective-permute-start | bytes 405512 | tf_op jit(solution)/shard_map/ppermute | solution.py:485
  73.5 7.3 %collective-permute-start.28 = (f32[256,128]{1,0:T(8,128)S(1)}, f32[256,128]{1,0:T(8,128)S(1)}, u32[]{:S(2)}, u32[]{:S(2)}) collective-permute-start(f32[256,128]{1,0:T(8,128)S(1)} %get-tuple-element.183), channel_id=1, source_target_pairs={{0,4},{4,0},{8,12},{12,8},{16,20},{20,16},{24,28},{28,24},{1,5},{5... | collective-permute-start | bytes 393224 | tf_op jit(solution)/shard_map/ppermute | solution.py:341
  73.6 10.5 %collective-permute-start.29 = (f32[256,128]{1,0:T(8,128)S(1)}, f32[256,128]{1,0:T(8,128)S(1)}, u32[]{:S(2)}, u32[]{:S(2)}) collective-permute-start(f32[256,128]{1,0:T(8,128)S(1)} %get-tuple-element.184), channel_id=1, source_target_pairs={{0,8},{4,12},{8,0},{12,4},{16,24},{20,28},{24,16},{28,20},{1,9},{5... | collective-permute-start | bytes 393224 | tf_op jit(solution)/shard_map/ppermute | solution.py:341
  74.0 10.1 %collective-permute-start.30 = (f32[256,128]{1,0:T(8,128)S(1)}, f32[256,128]{1,0:T(8,128)S(1)}, u32[]{:S(2)}, u32[]{:S(2)}) collective-permute-start(f32[256,128]{1,0:T(8,128)S(1)} %get-tuple-element.185), channel_id=1, source_target_pairs={{0,12},{4,8},{8,4},{12,0},{16,28},{20,24},{24,20},{28,16},{1,13},{... | collective-permute-start | bytes 393224 | tf_op jit(solution)/shard_map/ppermute | solution.py:341
  77.2 9.3 %collective-permute-start.25 = (f32[264,128]{1,0:T(8,128)S(1)}, f32[264,128]{1,0:T(8,128)S(1)}, u32[]{:S(2)}, u32[]{:S(2)}) collective-permute-start(f32[264,128]{1,0:T(8,128)S(1)} %get-tuple-element.168), channel_id=1, source_target_pairs={{0,4},{4,0},{8,12},{12,8},{16,20},{20,16},{24,28},{28,24},{1,5},{5... | collective-permute-start | bytes 405512 | tf_op jit(solution)/shard_map/ppermute | solution.py:341
  77.4 9.2 %collective-permute-start.26 = (f32[264,128]{1,0:T(8,128)S(1)}, f32[264,128]{1,0:T(8,128)S(1)}, u32[]{:S(2)}, u32[]{:S(2)}) collective-permute-start(f32[264,128]{1,0:T(8,128)S(1)} %get-tuple-element.169), channel_id=1, source_target_pairs={{0,8},{4,12},{8,0},{12,4},{16,24},{20,28},{24,16},{28,20},{1,9},{5... | collective-permute-start | bytes 405512 | tf_op jit(solution)/shard_map/ppermute | solution.py:341
  (11 other events, 69.7 us)
where the time goes:
time: 90 us; the launch traced here: 89.8 us
  Pallas kernels  39.7 us (44%)
  starting transfers between devices  37.3 us (41%)
  waiting for transfers between devices  11.6 us (13%)
  between operations  1.14 us (1%)
    pallas_call x32, Pallas kernels, call(): pl.pallas_call(run, name=name, out_shape=[o for o, _ in outs], in_specs=[...  39.7 us
    ppermute x24, starting transfers between devices, scatter(): lax.ppermute(pieces[d], 'seq', [(b, b ^ d) for b in range(count)])  26.5 us
    ppermute x24, waiting for transfers between devices, scatter(): lax.ppermute(pieces[d], 'seq', [(b, b ^ d) for b in range(count)])  9.4 us
    ppermute x4, starting transfers between devices, scan(): lax.ppermute(total, 'seq', [(b, b ^ quad) for b in range(count)])  9 us
    ppermute x4, waiting for transfers between devices, scan(): lax.ppermute(total, 'seq', [(b, b ^ quad) for b in range(count)])  2.18 us
    ppermute x3, starting transfers between devices, body(): lax.ppermute(sums, 'head', [(b, b ^ d) for b in range(head_n)])  1.89 us
  transfers between devices with their start and end apart: 31, of which 10 were waited for; matrix products, arithmetic and copies ran while one was open for 0% of the time, Pallas kernels for 34%

commit v1 on v0

--- a/solution.py
+++ b/solution.py
@@ -11,22 +11,19 @@
 EPS = 1e-06
 F32 = jnp.float32
 BF16 = jnp.bfloat16
-HIGH = lax.Precision.HIGHEST
 VMEM_LIMIT = 12 * 1024 * 1024
 VMEM = pl.BlockSpec(memory_space=pltpu.VMEM)
 SMEM = pl.BlockSpec(memory_space=pltpu.SMEM)
 HBM = pl.BlockSpec(memory_space=pltpu.HBM)
 ANY = pl.BlockSpec(memory_space=pl.ANY)
 INTRA_SHARE = [1, 0, 2, 0, 1]
-BACK_SHARE = [2, 2, 2, 0, 2]
+BACK_SHARE = [2, 3, 0, 1, 2]
 BACK_SIZE = 1
 LONG = 1 << 26
 
 
-def dot(a, b, ca, cb, precision=None):
-    return lax.dot_general(
-        a, b, (((ca,), (cb,)), ((), ())), precision=precision, preferred_element_type=F32
-    )
+def dot(a, b, ca, cb):
+    return lax.dot_general(a, b, (((ca,), (cb,)), ((), ())), preferred_element_type=F32)
 
 
 def shape(dims, dtype=F32):
@@ -171,20 +168,25 @@
     rest = refs[2 * sides + pieces_n :]
     before, out, attn_out = (None, *rest) if first else rest
     steps = pieces_n // sides
-    squares = cross = None
-    for d in range(pieces_n):
-        side, at = d // steps, d % steps
-        for h in range(hs):
-            cols = part(at * hs + h, HD)
-            prefix = pieces[d][part(h, HD), :].astype(BF16)
-            attn = intras[side][:, cols] + dot(q[:, head_at(chunk, pieces_n, d, hs, h)], prefix, 1, 0)
-            attn_out[:, part(d * hs + h, HD)] = attn
-            wide = weights[side][:, cols]
-            squares = attn * attn if squares is None else squares + attn * attn
-            cross = attn * wide if cross is None else cross + attn * wide
-    place = lax.broadcasted_iota(jnp.int32, (8, HD), 0)
-    total = dot((place == 0).astype(F32), squares, 1, 1, HIGH)
-    total = total + dot((place == 1).astype(F32), cross, 1, 1, HIGH)
+    rows = q.shape[0]
+    prefixes = [pieces[d][part(h, HD), :].astype(BF16) for d in range(pieces_n) for h in range(hs)]
+    sums = []
+    for r in range(0, rows, HD):
+        here = slice(r, r + HD)
+        squares = cross = None
+        for d in range(pieces_n):
+            side, at = d // steps, d % steps
+            for h in range(hs):
+                cols = part(at * hs + h, HD)
+                cols_q = head_at(chunk, pieces_n, d, hs, h)
+                attn = intras[side][here, cols] + dot(q[here, cols_q], prefixes[d * hs + h], 1, 0)
+                attn_out[here, part(d * hs + h, HD)] = attn
+                wide = weights[side][here, cols]
+                squares = attn * attn if squares is None else squares + attn * attn
+                cross = attn * wide if cross is None else cross + attn * wide
+        sums.append([jnp.sum(one.T, 0, keepdims=True) for one in (squares, cross)])
+    both = [jnp.concatenate([one[i] for one in sums], 1) for i in range(2)]
+    total = jnp.concatenate(both + [jnp.zeros((6, rows), F32)], 0)
     out[...] = total if first else total + before[...]
 
 
@@ -192,36 +194,44 @@
     weights, refs = refs[:sides], refs[sides:]
     parts, refs = refs[:parts_n], refs[parts_n:]
     gains_before, refs = refs[:carried], refs[carried:]
-    da, inverse = refs[:2]
-    outs = refs[2 : 2 + quad]
-    factor = refs[-1]
-    total = parts[0][...]
-    for one in parts[1:]:
-        total = total + one[...]
-    place = lax.broadcasted_iota(jnp.int32, (8, HD), 0)
-    mean = dot(total, (place == 0).astype(F32), 0, 0, HIGH) * (1.0 / full) + EPS
-    inverse[...] = lax.rsqrt(mean)
-    factor[...] = dot(total, (place == 1).astype(F32), 0, 0, HIGH) * (1.0 / full) / mean
+    if chunk == 0:
+        da, inverse, factor = refs[:3]
+        outs = refs[3 : 3 + quad]
+        total = parts[0][...]
+        for one in parts[1:]:
+            total = total + one[...]
+        mean = total[0:1] * (1.0 / full) + EPS
+        tall = (HD, total.shape[1])
+        inverse[...] = jnp.broadcast_to(lax.rsqrt(mean), tall).T
+        factor[...] = jnp.broadcast_to(total[1:2] * (1.0 / full) / mean, tall).T
+    else:
+        inverse, factor = parts
+        da, outs = refs[0], refs[1 : 1 + quad]
     steps = quad // sides
     sw = hs * HD
+    rows = queries.shape[0]
+    block = 64 if rows % 64 == 0 else rows
+    sums = [None] * (quad * hs)
+    for r in range(0, rows, block):
+        here = slice(r, r + block)
+        scale, taken = inverse[here, :], factor[here, :]
+        for i in range(quad * hs):
+            side, at = i // (steps * hs), i % (steps * hs)
+            attn, wide = attns[here, part(i, HD)], weights[side][here, part(at, HD)]
+            da[here, part(i, HD)] = ((wide - attn * taken) * scale).astype(BF16)
+            one = jnp.sum((wide * attn * scale).reshape(block // 8, 8, HD), 0)
+            sums[i] = one if sums[i] is None else sums[i] + one
+    gains = [jnp.sum(one, 0, keepdims=True) for one in sums]
     for d in range(quad):
-        side, at = d // steps, d % steps
-        rows_out = []
-        for h in range(hs):
-            mine = part(d * hs + h, HD)
-            attn = attns[:, mine]
-            wide = weights[side][:, part(at * hs + h, HD)]
-            scale = inverse[...]
-            da[:, mine] = ((wide - attn * factor[...]) * scale).astype(BF16)
-            rows_out.append(jnp.sum(wide * attn * scale, 0, keepdims=True))
         write_states(outs[d], queries[:, shard_cols(chunk, quad, d, sw)], da[:, part(d, sw)], hs)
+        rows_out = gains[d * hs : (d + 1) * hs]
         if last:
             older = [g[part(d, hs), :] for g in gains_before]
             pad = outs[d].shape[0] - sw - (len(older) + 1) * hs
             zero = [jnp.zeros((pad, HD), F32)] if pad else []
             outs[d][sw:, :] = jnp.concatenate(older + rows_out + zero, 0)
         else:
-            refs[2 + quad][part(d, hs), :] = jnp.concatenate(rows_out, 0)
+            refs[-1][part(d, hs), :] = jnp.concatenate(rows_out, 0)
 
 
 def total_kernel(sw, pieces_n, whole, *refs):
@@ -292,6 +302,16 @@
             ggate[:, mine] = (weight[:, part(in_side, HD)] * attns[:, cols] * inverse[...] * (1.0 - sig)).astype(BF16)
 
 
+def diagonals(piece, hs, at, d):
+    sw = hs * HD
+    if hs == 2:
+        zero = jnp.zeros((HD, HD), BF16)
+        one, two = piece[:HD, :].astype(BF16), piece[HD:sw, :].astype(BF16)
+        both = jnp.concatenate([jnp.concatenate([one, zero], 1), jnp.concatenate([zero, two], 1)], 0)
+        return [(part(at, sw), part(d, sw), both)]
+    return [(part(at * hs + h, HD), part(d * hs + h, HD), piece[part(h, HD), :].astype(BF16)) for h in range(hs)]
+
+
 def finish_kernel(hs, quad, chunk, chunks, sizes, olds, last, k, v, *rest):
     n = len(sizes)
     sw = hs * HD
@@ -316,15 +336,6 @@
         i, at = where[d]
         store(d, 0, gq_parts[i].at[:, part(at, sw)], gq)
         store(d, 1, ggate_parts[i].at[:, part(at, sw)], ggate)
-    for d in range(quad):
-        i, at = where[d]
-        for h in range(hs):
-            mine, cols = part(at * hs + h, HD), part(d * hs + h, HD)
-            suffix = pieces[d][part(h, HD), :].astype(BF16)
-            gk_out[:, cols] = (gk_parts[i][:, mine] + dot(v[:, cols], suffix, 1, 1)).astype(BF16)
-            gv_out[:, cols] = (gv_parts[i][:, mine] + dot(k[:, cols], suffix, 1, 0)).astype(BF16)
-        store(d, 2, gk_out.at[:, part(d, sw)], gk)
-        store(d, 3, gv_out.at[:, part(d, sw)], gv)
     if last:
         for c in range(chunks):
             for d in range(quad):
@@ -332,6 +343,13 @@
                     at = head_at(c, quad, d, hs, h)
                     row = sw + c * hs + h
                     ggain[:, at] = pieces[d][row : row + 1, :] / gain[:, at]
+    for d in range(quad):
+        i, at = where[d]
+        for mine, cols, suffix in diagonals(pieces[d], hs, at, d):
+            gk_out[:, cols] = (gk_parts[i][:, mine] + dot(v[:, cols], suffix, 1, 1)).astype(BF16)
+            gv_out[:, cols] = (gv_parts[i][:, mine] + dot(k[:, cols], suffix, 1, 0)).astype(BF16)
+        store(d, 2, gk_out.at[:, part(d, sw)], gk)
+        store(d, 3, gv_out.at[:, part(d, sw)], gv)
     for copy in copies:
         copy.wait()
 
@@ -415,15 +433,15 @@
 
     def adjoints(c, attn, parts, gains, after):
         last = c == final
-        outs = [(shape((rows, cw), BF16), VMEM), (shape((rows, HD)), VMEM)]
+        outs = [(shape((rows, cw), BF16), VMEM)] + ([(shape((rows, HD)), VMEM)] * 2 if c == 0 else [])
         outs += [(shape((sw + (pad if last else 0), HD)), VMEM)] * quad
         if not last:
             outs += [(shape((quad * hs, HD)), VMEM)]
         return call(
-            functools.partial(adjoint_kernel, hs, c, full, sides, quad, head_n, len(gains), last), "adjoints",
+            functools.partial(adjoint_kernel, hs, c, full, sides, quad, len(parts), len(gains), last), "adjoints",
             [(queries, VMEM), (attn, VMEM)] + [(lot[1], VMEM) for lot in lots[c]] + [(p, VMEM) for p in parts]
             + [(g, VMEM) for g in gains],
-            outs, [pltpu.VMEM((rows, HD), F32)], after,
+            outs, [], after,
         )
 
     def probabilities(c, side, k, after):
@@ -544,7 +562,9 @@
 
     das, messages, gains = [], [], []
     for c in every:
-        da, inverse, *pieces = adjoints(c, attns[c], parts, gains if c == final else [], after)
+        da, *pieces = adjoints(c, attns[c], parts if c == 0 else scales, gains if c == final else [], after)
+        if c == 0:
+            scales, pieces = pieces[:2], pieces[2:]
         after = []
         das.append(da)
         messages.append(pieces[:quad])
@@ -555,7 +575,7 @@
 
     def back_jobs(window, after):
         for c, d in back_lots[window]:
-            halves[c].append(back(c, d, size, *kv[c], das[c], inverse, prefix[c], after))
+            halves[c].append(back(c, d, size, *kv[c], das[c], scales[0], prefix[c], after))
             after = halves[c][-1][2:3]
         return after
 

time: 90 us -> 85.7 us (0.952)
  waiting for transfers between devices: 11.6 us -> 7 us
  starting transfers between devices: 37.3 us -> 40.3 us
  Pallas kernels: 39.7 us -> 37 us
    ppermute x24, starting transfers between devices: 26.5 us -> 29.4 us  [scatter(): lax.ppermute(pieces[d], 'seq', [(b, b ^ d) for b in range(count)])]
    pallas_call x32, Pallas kernels: 39.7 us -> 37 us  [call(): pl.pallas_call(run, name=name, out_shape=[o for o, _ in outs], in_specs=[...]
    ppermute x24, waiting for transfers between devices: 9.4 us -> 6.72 us  [scatter(): lax.ppermute(pieces[d], 'seq', [(b, b ^ d) for b in range(count)])]
    ppermute x4, waiting for transfers between devices: 2.18 us -> 0.27 us  [scan(): lax.ppermute(total, 'seq', [(b, b ^ quad) for b in range(count)])]
  transfers between devices with their start and end apart: 31 -> 31, of which waited for: 10 -> 8; matrix products, arithmetic and copies ran while one was open for 0% -> 0% of each run, Pallas kernels for 34% -> 34%
where the time goes in v1:
time: 85.7 us; the launch traced here: 85.5 us
  starting transfers between devices  40.3 us (47%)
  Pallas kernels  37 us (43%)
  waiting for transfers between devices  7 us (8%)
  between operations  1.17 us (1%)
    pallas_call x32, Pallas kernels, call(): pl.pallas_call(run, name=name, out_shape=[o for o, _ in outs], in_specs=[...  37 us
    ppermute x24, starting transfers between devices, scatter(): lax.ppermute(pieces[d], 'seq', [(b, b ^ d) for b in range(count)])  29.4 us
    ppermute x4, starting transfers between devices, scan(): lax.ppermute(total, 'seq', [(b, b ^ quad) for b in range(count)])  8.99 us
    ppermute x24, waiting for transfers between devices, scatter(): lax.ppermute(pieces[d], 'seq', [(b, b ^ d) for b in range(count)])  6.72 us
    ppermute x3, starting transfers between devices, body(): lax.ppermute(sums, 'head', [(b, b ^ d) for b in range(head_n)])  1.92 us
  transfers between devices with their start and end apart: 31, of which 8 were waited for; matrix products, arithmetic and copies ran while one was open for 0% of the time, Pallas kernels for 34%

profile of v1, /device:TPU:0, one launch (start us, length us, event | category | flops | bytes accessed | tf_op | source)
XLA Modules:
  0.0 85.5 jit_solution(11959859723297033116)
XLA Ops:
  0.6 2.5 %states.2 = (bf16[512,1024]{1,0:T(8,128)(2,1)S(1)}, bf16[512,1024]{1,0:T(8,128)(2,1)S(1)}, f32[256,128]{1,0:T(8,128)S(1)}, f32[256,128]{1,0:T(8,128)S(1)}, f32[2...) custom-call(bf16[512,2048]{1,0:T(8,128)(2,1)} %refs_0_.7, ...), custom_call_target="tpu_custom_call" | custom-call | flops 1 | bytes 1 | tf_op jit(solution)/shard_map/states/pallas_call | solution.py:39
  3.2 3.0 %collective-permute-start.3 = (f32[256,128]{1,0:T(8,128)S(1)}, f32[256,128]{1,0:T(8,128)S(1)}, u32[]{:S(2)}, u32[]{:S(2)}) collective-permute-start(f32[256,128]{1,0:T(8,128)S(1)} %get-tuple-element.111), channel_id=1, source_target_pairs={{0,4},{4,0},{8,12},{12,8},{16,20},{20,16},{24,28},{28,24},{1,5},{5... | collective-permute-start | bytes 393224 | tf_op jit(solution)/shard_map/ppermute | solution.py:359
  6.2 1.6 %collective-permute-start.4 = (f32[256,128]{1,0:T(8,128)S(1)}, f32[256,128]{1,0:T(8,128)S(1)}, u32[]{:S(2)}, u32[]{:S(2)}) collective-permute-start(f32[256,128]{1,0:T(8,128)S(1)} %get-tuple-element.112), channel_id=1, source_target_pairs={{0,8},{4,12},{8,0},{12,4},{16,24},{20,28},{24,16},{28,20},{1,9},{5... | collective-permute-start | bytes 393224 | tf_op jit(solution)/shard_map/ppermute | solution.py:359
  7.8 2.5 %states.3 = (bf16[512,1024]{1,0:T(8,128)(2,1)S(1)}, bf16[512,1024]{1,0:T(8,128)(2,1)S(1)}, f32[256,128]{1,0:T(8,128)S(1)}, f32[256,128]{1,0:T(8,128)S(1)}, f32[2...) custom-call(bf16[512,2048]{1,0:T(8,128)(2,1)} %refs_0_.7, bf16[512,2048]{1,0:T(8,128)(2,1)} %refs_1_.7, ...), custom_call_target="tpu_custom_call" | custom-call | flops 1 | bytes 1 | tf_op jit(solution)/shard_map/states/pallas_call | solution.py:39
  10.4 2.0 %collective-permute-start = (f32[256,128]{1,0:T(8,128)S(1)}, f32[256,128]{1,0:T(8,128)S(1)}, u32[]{:S(2)}, u32[]{:S(2)}) collective-permute-start(f32[256,128]{1,0:T(8,128)S(1)} %get-tuple-element.108), channel_id=1, source_target_pairs={{0,4},{4,0},{8,12},{12,8},{16,20},{20,16},{24,28},{28,24},{1,5},{5... | collective-permute-start | bytes 393224 | tf_op jit(solution)/shard_map/ppermute | solution.py:359
  12.3 1.6 %collective-permute-start.1 = (f32[256,128]{1,0:T(8,128)S(1)}, f32[256,128]{1,0:T(8,128)S(1)}, u32[]{:S(2)}, u32[]{:S(2)}) collective-permute-start(f32[256,128]{1,0:T(8,128)S(1)} %get-tuple-element.109), channel_id=1, source_target_pairs={{0,8},{4,12},{8,0},{12,4},{16,24},{20,28},{24,16},{28,20},{1,9},{5... | collective-permute-start | bytes 393224 | tf_op jit(solution)/shard_map/ppermute | solution.py:359
  15.5 3.0 %collective-permute-start.7 = (f32[256,128]{1,0:T(8,128)S(1)}, f32[256,128]{1,0:T(8,128)S(1)}, u32[]{:S(2)}, u32[]{:S(2)}) collective-permute-start(f32[256,128]{1,0:T(8,128)S(1)} %total.4.refs_4_), channel_id=1, source_target_pairs={{0,16},{4,20},{8,24},{12,28},{16,0},{20,4},{24,8},{28,12},{1,17},{... | collective-permute-start | bytes 393224 | tf_op jit(solution)/shard_map/ppermute | solution.py:503
  21.2 2.9 %collective-permute-start.6 = (f32[256,128]{1,0:T(8,128)S(1)}, f32[256,128]{1,0:T(8,128)S(1)}, u32[]{:S(2)}, u32[]{:S(2)}) collective-permute-start(f32[256,128]{1,0:T(8,128)S(1)} %total.5.refs_7_), channel_id=1, source_target_pairs={{0,16},{4,20},{8,24},{12,28},{16,0},{20,4},{24,8},{28,12},{1,17},{... | collective-permute-start | bytes 393224 | tf_op jit(solution)/shard_map/ppermute | solution.py:503
  27.3 1.6 %collective-permute-start.11 = (f32[256,128]{1,0:T(8,128)S(1)}, f32[256,128]{1,0:T(8,128)S(1)}, u32[]{:S(2)}, u32[]{:S(2)}) collective-permute-start(f32[256,128]{1,0:T(8,128)S(1)} %get-tuple-element.127), channel_id=1, source_target_pairs={{0,4},{4,0},{8,12},{12,8},{16,20},{20,16},{24,28},{28,24},{1,5},{5... | collective-permute-start | bytes 393224 | tf_op jit(solution)/shard_map/ppermute | solution.py:359
  28.8 1.6 %collective-permute-start.12 = (f32[256,128]{1,0:T(8,128)S(1)}, f32[256,128]{1,0:T(8,128)S(1)}, u32[]{:S(2)}, u32[]{:S(2)}) collective-permute-start(f32[256,128]{1,0:T(8,128)S(1)} %get-tuple-element.128), channel_id=1, source_target_pairs={{0,8},{4,12},{8,0},{12,4},{16,24},{20,28},{24,16},{28,20},{1,9},{5... | collective-permute-start | bytes 393224 | tf_op jit(solution)/shard_map/ppermute | solution.py:359
  31.0 1.6 %collective-permute-start.8 = (f32[256,128]{1,0:T(8,128)S(1)}, f32[256,128]{1,0:T(8,128)S(1)}, u32[]{:S(2)}, u32[]{:S(2)}) collective-permute-start(f32[256,128]{1,0:T(8,128)S(1)} %get-tuple-element.122), channel_id=1, source_target_pairs={{0,4},{4,0},{8,12},{12,8},{16,20},{20,16},{24,28},{28,24},{1,5},{5... | collective-permute-start | bytes 393224 | tf_op jit(solution)/shard_map/ppermute | solution.py:359
  41.8 1.6 %collective-permute-start.15 = (f32[8,512]{1,0:T(8,128)S(1)}, f32[8,512]{1,0:T(8,128)S(1)}, u32[]{:S(2)}, u32[]{:S(2)}) collective-permute-start(f32[8,512]{1,0:T(8,128)S(1)} %get-tuple-element.133.refs_3_.refs_4_), channel_id=1, source_target_pairs={{0,2},{1,3},{2,0},{3,1},{4,6},{5,7},{6,4},{7,5},{8,10},{9,11},{10,... | collective-permute-start | bytes 49160 | tf_op jit(solution)/shard_map/ppermute | solution.py:557
  55.7 1.6 %back.8 = (bf16[512,256]{1,0:T(8,128)(2,1)S(1)}, bf16[512,256]{1,0:T(8,128)(2,1)S(1)}, f32[512,256]{1,0:T(8,128)S(1)}, f32[512,256]{1,0:T(8,128)S(1)}) custom-call(bf16[512,1024]{1,0:T(8,128)(2,1)S(1)} %get-tuple-element.105.refs_0_, bf16[512,1024]{1,0:T(8,128)(2,1)S(1)} %get-tuple-element.106.refs_1_, bf16[512,1024]{1,0:T(8,128)(2,1)S(1)} %get-tuple-element.139.refs_2_, ...), custom_call_target="tpu_custom_call" | custom-call | flops 1 | bytes 1 | tf_op jit(solution)/shard_map/back/pallas_call | solution.py:39
  57.4 1.6 %back.9 = (bf16[512,256]{1,0:T(8,128)(2,1)S(1)}, bf16[512,256]{1,0:T(8,128)(2,1)S(1)}, f32[512,256]{1,0:T(8,128)S(1)}, f32[512,256]{1,0:T(8,128)S(1)}) custom-call(bf16[512,1024]{1,0:T(8,128)(2,1)S(1)} %get-tuple-element.105.refs_0_, bf16[512,1024]{1,0:T(8,128)(2,1)S(1)} %get-tuple-element.106.refs_1_, bf16[512,1024]{1,0:T(8,128)(2,1)S(1)} %get-tuple-element.139.refs_2_, ...), custom_call_target="tpu_custom_call" | custom-call | flops 1 | bytes 1 | tf_op jit(solution)/shard_map/back/pallas_call | solution.py:39
  60.4 1.6 %back.10 = (bf16[512,256]{1,0:T(8,128)(2,1)S(1)}, bf16[512,256]{1,0:T(8,128)(2,1)S(1)}, f32[512,256]{1,0:T(8,128)S(1)}, f32[512,256]{1,0:T(8,128)S(1)}) custom-call(bf16[512,1024]{1,0:T(8,128)(2,1)S(1)} %get-tuple-element.105.refs_0_, bf16[512,1024]{1,0:T(8,128)(2,1)S(1)} %get-tuple-element.106.refs_1_, bf16[512,1024]{1,0:T(8,128)(2,1)S(1)} %get-tuple-element.139.refs_2_, ...), custom_call_target="tpu_custom_call" | custom-call | flops 1 | bytes 1 | tf_op jit(solution)/shard_map/back/pallas_call | solution.py:39
  62.1 1.6 %back.11 = (bf16[512,256]{1,0:T(8,128)(2,1)S(1)}, bf16[512,256]{1,0:T(8,128)(2,1)S(1)}, f32[512,256]{1,0:T(8,128)S(1)}, f32[512,256]{1,0:T(8,128)S(1)}) custom-call(bf16[512,1024]{1,0:T(8,128)(2,1)S(1)} %get-tuple-element.105.refs_0_, bf16[512,1024]{1,0:T(8,128)(2,1)S(1)} %get-tuple-element.106.refs_1_, bf16[512,1024]{1,0:T(8,128)(2,1)S(1)} %get-tuple-element.139.refs_2_, ...), custom_call_target="tpu_custom_call" | custom-call | flops 1 | bytes 1 | tf_op jit(solution)/shard_map/back/pallas_call | solution.py:39
  63.7 1.6 %back.12 = (bf16[512,256]{1,0:T(8,128)(2,1)S(1)}, bf16[512,256]{1,0:T(8,128)(2,1)S(1)}, f32[512,256]{1,0:T(8,128)S(1)}, f32[512,256]{1,0:T(8,128)S(1)}) custom-call(bf16[512,1024]{1,0:T(8,128)(2,1)S(1)} %get-tuple-element.102.refs_0_, bf16[512,1024]{1,0:T(8,128)(2,1)S(1)} %get-tuple-element.103.refs_1_, bf16[512,1024]{1,0:T(8,128)(2,1)S(1)} %get-tuple-element.138.refs_2_, ...), custom_call_target="tpu_custom_call" | custom-call | flops 1 | bytes 1 | tf_op jit(solution)/shard_map/back/pallas_call | solution.py:39
  65.4 1.7 %collective-permute-start.24 = (f32[264,128]{1,0:T(8,128)S(1)}, f32[264,128]{1,0:T(8,128)S(1)}, u32[]{:S(2)}, u32[]{:S(2)}) collective-permute-start(f32[264,128]{1,0:T(8,128)S(1)} %total.7.refs_5_), channel_id=1, source_target_pairs={{0,16},{4,20},{8,24},{12,28},{16,0},{20,4},{24,8},{28,12},{1,17},{... | collective-permute-start | bytes 405512 | tf_op jit(solution)/shard_map/ppermute | solution.py:503
  71.1 1.8 %back.13 = (bf16[512,256]{1,0:T(8,128)(2,1)S(1)}, bf16[512,256]{1,0:T(8,128)(2,1)S(1)}, f32[512,256]{1,0:T(8,128)S(1)}, f32[512,256]{1,0:T(8,128)S(1)}) custom-call(bf16[512,1024]{1,0:T(8,128)(2,1)S(1)} %get-tuple-element.102.refs_0_, bf16[512,1024]{1,0:T(8,128)(2,1)S(1)} %get-tuple-element.103.refs_1_, bf16[512,1024]{1,0:T(8,128)(2,1)S(1)} %get-tuple-element.138.refs_2_, ...), custom_call_target="tpu_custom_call" | custom-call | flops 1 | bytes 1 | tf_op jit(solution)/shard_map/back/pallas_call | solution.py:39
  74.3 1.9 %collective-permute-start.26 = (f32[264,128]{1,0:T(8,128)S(1)}, f32[264,128]{1,0:T(8,128)S(1)}, u32[]{:S(2)}, u32[]{:S(2)}) collective-permute-start(f32[264,128]{1,0:T(8,128)S(1)} %get-tuple-element.171), channel_id=1, source_target_pairs={{0,8},{4,12},{8,0},{12,4},{16,24},{20,28},{24,16},{28,20},{1,9},{5... | collective-permute-start | bytes 405512 | tf_op jit(solution)/shard_map/ppermute | solution.py:359
  76.6 1.6 %back.14 = (bf16[512,256]{1,0:T(8,128)(2,1)S(1)}, bf16[512,256]{1,0:T(8,128)(2,1)S(1)}, f32[512,256]{1,0:T(8,128)S(1)}, f32[512,256]{1,0:T(8,128)S(1)}) custom-call(bf16[512,1024]{1,0:T(8,128)(2,1)S(1)} %get-tuple-element.102.refs_0_, bf16[512,1024]{1,0:T(8,128)(2,1)S(1)} %get-tuple-element.103.refs_1_, bf16[512,1024]{1,0:T(8,128)(2,1)S(1)} %get-tuple-element.138.refs_2_, ...), custom_call_target="tpu_custom_call" | custom-call | flops 1 | bytes 1 | tf_op jit(solution)/shard_map/back/pallas_call | solution.py:39
  78.3 1.6 %back.15 = (bf16[512,256]{1,0:T(8,128)(2,1)S(1)}, bf16[512,256]{1,0:T(8,128)(2,1)S(1)}, f32[512,256]{1,0:T(8,128)S(1)}, f32[512,256]{1,0:T(8,128)S(1)}) custom-call(bf16[512,1024]{1,0:T(8,128)(2,1)S(1)} %get-tuple-element.102.refs_0_, bf16[512,1024]{1,0:T(8,128)(2,1)S(1)} %get-tuple-element.103.refs_1_, bf16[512,1024]{1,0:T(8,128)(2,1)S(1)} %get-tuple-element.138.refs_2_, ...), custom_call_target="tpu_custom_call" | custom-call | flops 1 | bytes 1 | tf_op jit(solution)/shard_map/back/pallas_call | solution.py:39
  79.9 2.4 %finish.2 = (bf16[512,2048]{1,0:T(8,128)(2,1)}, bf16[512,2048]{1,0:T(8,128)(2,1)}, bf16[512,2048]{1,0:T(8,128)(2,1)}, bf16[512,2048]{1,0:T(8,128)(2,1)}) custom-call(bf16[512,1024]{1,0:T(8,128)(2,1)S(1)} %get-tuple-element.105.refs_0_, bf16[512,1024]{1,0:T(8,128)(2,1)S(1)} %get-tuple-element.106.refs_1_, bf16[512,256]{1,0:T(8,128)(2,1)S(1)} %get-tuple-element.173.refs_2_, ...), custom_call_target="tpu_custom_call" | custom-call | flops 67108864 | bytes 67108864 | tf_op jit(solution)/shard_map/finish/pallas_call | solution.py:39
  82.4 3.0 %finish.3 = (bf16[512,2048]{1,0:T(8,128)(2,1)}, bf16[512,2048]{1,0:T(8,128)(2,1)}, bf16[512,2048]{1,0:T(8,128)(2,1)}, bf16[512,2048]{1,0:T(8,128)(2,1)}, f32[1,2048]{1,0:T(1,128)}) custom-call(bf16[512,1024]{1,0:T(8,128)(2,1)S(1)} %get-tuple-element.102.refs_0_, ...), custom_call_target="tpu_custom_call", output_to_operand_aliasing={{0}: (23, {}), {1}: (24, {}), {2}: (25, {}), {3}: (26, {})} | custom-call | flops 67108864 | bytes 67108864 | tf_op jit(solution)/shard_map/finish/pallas_call | solution.py:39
  (78 shorter events, 36.6 us)
Async XLA Ops:
  3.2 10.7 %collective-permute-start.3 = (f32[256,128]{1,0:T(8,128)S(1)}, f32[256,128]{1,0:T(8,128)S(1)}, u32[]{:S(2)}, u32[]{:S(2)}) collective-permute-start(f32[256,128]{1,0:T(8,128)S(1)} %get-tuple-element.111), channel_id=1, source_target_pairs={{0,4},{4,0},{8,12},{12,8},{16,20},{20,16},{24,28},{28,24},{1,5},{5... | collective-permute-start | bytes 393224 | tf_op jit(solution)/shard_map/ppermute | solution.py:359
  6.2 9.2 %collective-permute-start.4 = (f32[256,128]{1,0:T(8,128)S(1)}, f32[256,128]{1,0:T(8,128)S(1)}, u32[]{:S(2)}, u32[]{:S(2)}) collective-permute-start(f32[256,128]{1,0:T(8,128)S(1)} %get-tuple-element.112), channel_id=1, source_target_pairs={{0,8},{4,12},{8,0},{12,4},{16,24},{20,28},{24,16},{28,20},{1,9},{5... | collective-permute-start | bytes 393224 | tf_op jit(solution)/shard_map/ppermute | solution.py:359
  7.8 7.6 %collective-permute-start.5 = (f32[256,128]{1,0:T(8,128)S(1)}, f32[256,128]{1,0:T(8,128)S(1)}, u32[]{:S(2)}, u32[]{:S(2)}) collective-permute-start(f32[256,128]{1,0:T(8,128)S(1)} %get-tuple-element.113), channel_id=1, source_target_pairs={{0,12},{4,8},{8,4},{12,0},{16,28},{20,24},{24,20},{28,16},{1,13},{... | collective-permute-start | bytes 393224 | tf_op jit(solution)/shard_map/ppermute | solution.py:359
  10.4 8.2 %collective-permute-start = (f32[256,128]{1,0:T(8,128)S(1)}, f32[256,128]{1,0:T(8,128)S(1)}, u32[]{:S(2)}, u32[]{:S(2)}) collective-permute-start(f32[256,128]{1,0:T(8,128)S(1)} %get-tuple-element.108), channel_id=1, source_target_pairs={{0,4},{4,0},{8,12},{12,8},{16,20},{20,16},{24,28},{28,24},{1,5},{5... | collective-permute-start | bytes 393224 | tf_op jit(solution)/shard_map/ppermute | solution.py:359
  12.3 7.3 %collective-permute-start.1 = (f32[256,128]{1,0:T(8,128)S(1)}, f32[256,128]{1,0:T(8,128)S(1)}, u32[]{:S(2)}, u32[]{:S(2)}) collective-permute-start(f32[256,128]{1,0:T(8,128)S(1)} %get-tuple-element.109), channel_id=1, source_target_pairs={{0,8},{4,12},{8,0},{12,4},{16,24},{20,28},{24,16},{28,20},{1,9},{5... | collective-permute-start | bytes 393224 | tf_op jit(solution)/shard_map/ppermute | solution.py:359
  13.9 7.3 %collective-permute-start.2 = (f32[256,128]{1,0:T(8,128)S(1)}, f32[256,128]{1,0:T(8,128)S(1)}, u32[]{:S(2)}, u32[]{:S(2)}) collective-permute-start(f32[256,128]{1,0:T(8,128)S(1)} %get-tuple-element.110), channel_id=1, source_target_pairs={{0,12},{4,8},{8,4},{12,0},{16,28},{20,24},{24,20},{28,16},{1,13},{... | collective-permute-start | bytes 393224 | tf_op jit(solution)/shard_map/ppermute | solution.py:359
  15.5 11.6 %collective-permute-start.7 = (f32[256,128]{1,0:T(8,128)S(1)}, f32[256,128]{1,0:T(8,128)S(1)}, u32[]{:S(2)}, u32[]{:S(2)}) collective-permute-start(f32[256,128]{1,0:T(8,128)S(1)} %total.4.refs_4_), channel_id=1, source_target_pairs={{0,16},{4,20},{8,24},{12,28},{16,0},{20,4},{24,8},{28,12},{1,17},{... | collective-permute-start | bytes 393224 | tf_op jit(solution)/shard_map/ppermute | solution.py:503
  21.2 9.6 %collective-permute-start.6 = (f32[256,128]{1,0:T(8,128)S(1)}, f32[256,128]{1,0:T(8,128)S(1)}, u32[]{:S(2)}, u32[]{:S(2)}) collective-permute-start(f32[256,128]{1,0:T(8,128)S(1)} %total.5.refs_7_), channel_id=1, source_target_pairs={{0,16},{4,20},{8,24},{12,28},{16,0},{20,4},{24,8},{28,12},{1,17},{... | collective-permute-start | bytes 393224 | tf_op jit(solution)/shard_map/ppermute | solution.py:503
  27.3 7.7 %collective-permute-start.11 = (f32[256,128]{1,0:T(8,128)S(1)}, f32[256,128]{1,0:T(8,128)S(1)}, u32[]{:S(2)}, u32[]{:S(2)}) collective-permute-start(f32[256,128]{1,0:T(8,128)S(1)} %get-tuple-element.127), channel_id=1, source_target_pairs={{0,4},{4,0},{8,12},{12,8},{16,20},{20,16},{24,28},{28,24},{1,5},{5... | collective-permute-start | bytes 393224 | tf_op jit(solution)/shard_map/ppermute | solution.py:359
  28.8 7.9 %collective-permute-start.12 = (f32[256,128]{1,0:T(8,128)S(1)}, f32[256,128]{1,0:T(8,128)S(1)}, u32[]{:S(2)}, u32[]{:S(2)}) collective-permute-start(f32[256,128]{1,0:T(8,128)S(1)} %get-tuple-element.128), channel_id=1, source_target_pairs={{0,8},{4,12},{8,0},{12,4},{16,24},{20,28},{24,16},{28,20},{1,9},{5... | collective-permute-start | bytes 393224 | tf_op jit(solution)/shard_map/ppermute | solution.py:359
  30.4 7.4 %collective-permute-start.13 = (f32[256,128]{1,0:T(8,128)S(1)}, f32[256,128]{1,0:T(8,128)S(1)}, u32[]{:S(2)}, u32[]{:S(2)}) collective-permute-start(f32[256,128]{1,0:T(8,128)S(1)} %get-tuple-element.129), channel_id=1, source_target_pairs={{0,12},{4,8},{8,4},{12,0},{16,28},{20,24},{24,20},{28,16},{1,13},{... | collective-permute-start | bytes 393224 | tf_op jit(solution)/shard_map/ppermute | solution.py:359
  31.0 8.3 %collective-permute-start.8 = (f32[256,128]{1,0:T(8,128)S(1)}, f32[256,128]{1,0:T(8,128)S(1)}, u32[]{:S(2)}, u32[]{:S(2)}) collective-permute-start(f32[256,128]{1,0:T(8,128)S(1)} %get-tuple-element.122), channel_id=1, source_target_pairs={{0,4},{4,0},{8,12},{12,8},{16,20},{20,16},{24,28},{28,24},{1,5},{5... | collective-permute-start | bytes 393224 | tf_op jit(solution)/shard_map/ppermute | solution.py:359
  49.1 9.9 %collective-permute-start.18 = (f32[256,128]{1,0:T(8,128)S(1)}, f32[256,128]{1,0:T(8,128)S(1)}, u32[]{:S(2)}, u32[]{:S(2)}) collective-permute-start(f32[256,128]{1,0:T(8,128)S(1)} %get-tuple-element.142), channel_id=1, source_target_pairs={{0,8},{4,12},{8,0},{12,4},{16,24},{20,28},{24,16},{28,20},{1,9},{5... | collective-permute-start | bytes 393224 | tf_op jit(solution)/shard_map/ppermute | solution.py:359
  50.0 9.0 %collective-permute-start.19 = (f32[256,128]{1,0:T(8,128)S(1)}, f32[256,128]{1,0:T(8,128)S(1)}, u32[]{:S(2)}, u32[]{:S(2)}) collective-permute-start(f32[256,128]{1,0:T(8,128)S(1)} %get-tuple-element.143), channel_id=1, source_target_pairs={{0,12},{4,8},{8,4},{12,0},{16,28},{20,24},{24,20},{28,16},{1,13},{... | collective-permute-start | bytes 393224 | tf_op jit(solution)/shard_map/ppermute | solution.py:359
  52.2 13.2 %collective-permute-start.21 = (f32[264,128]{1,0:T(8,128)S(1)}, f32[264,128]{1,0:T(8,128)S(1)}, u32[]{:S(2)}, u32[]{:S(2)}) collective-permute-start(f32[264,128]{1,0:T(8,128)S(1)} %get-tuple-element.150), channel_id=1, source_target_pairs={{0,4},{4,0},{8,12},{12,8},{16,20},{20,16},{24,28},{28,24},{1,5},{5... | collective-permute-start | bytes 405512 | tf_op jit(solution)/shard_map/ppermute | solution.py:359
  53.7 11.6 %collective-permute-start.22 = (f32[264,128]{1,0:T(8,128)S(1)}, f32[264,128]{1,0:T(8,128)S(1)}, u32[]{:S(2)}, u32[]{:S(2)}) collective-permute-start(f32[264,128]{1,0:T(8,128)S(1)} %get-tuple-element.151), channel_id=1, source_target_pairs={{0,8},{4,12},{8,0},{12,4},{16,24},{20,28},{24,16},{28,20},{1,9},{5... | collective-permute-start | bytes 405512 | tf_op jit(solution)/shard_map/ppermute | solution.py:359
  54.7 10.7 %collective-permute-start.23 = (f32[264,128]{1,0:T(8,128)S(1)}, f32[264,128]{1,0:T(8,128)S(1)}, u32[]{:S(2)}, u32[]{:S(2)}) collective-permute-start(f32[264,128]{1,0:T(8,128)S(1)} %get-tuple-element.152), channel_id=1, source_target_pairs={{0,12},{4,8},{8,4},{12,0},{16,28},{20,24},{24,20},{28,16},{1,13},{... | collective-permute-start | bytes 405512 | tf_op jit(solution)/shard_map/ppermute | solution.py:359
  59.1 8.3 %collective-permute-start.20 = (f32[256,128]{1,0:T(8,128)S(1)}, f32[256,128]{1,0:T(8,128)S(1)}, u32[]{:S(2)}, u32[]{:S(2)}) collective-permute-start(f32[256,128]{1,0:T(8,128)S(1)} %total.6.refs_12_), channel_id=1, source_target_pairs={{0,16},{4,20},{8,24},{12,28},{16,0},{20,4},{24,8},{28,12},{1,17},{... | collective-permute-start | bytes 393224 | tf_op jit(solution)/shard_map/ppermute | solution.py:503
  65.4 7.5 %collective-permute-start.24 = (f32[264,128]{1,0:T(8,128)S(1)}, f32[264,128]{1,0:T(8,128)S(1)}, u32[]{:S(2)}, u32[]{:S(2)}) collective-permute-start(f32[264,128]{1,0:T(8,128)S(1)} %total.7.refs_5_), channel_id=1, source_target_pairs={{0,16},{4,20},{8,24},{12,28},{16,0},{20,4},{24,8},{28,12},{1,17},{... | collective-permute-start | bytes 405512 | tf_op jit(solution)/shard_map/ppermute | solution.py:503
  67.5 8.7 %collective-permute-start.28 = (f32[256,128]{1,0:T(8,128)S(1)}, f32[256,128]{1,0:T(8,128)S(1)}, u32[]{:S(2)}, u32[]{:S(2)}) collective-permute-start(f32[256,128]{1,0:T(8,128)S(1)} %get-tuple-element.185), channel_id=1, source_target_pairs={{0,4},{4,0},{8,12},{12,8},{16,20},{20,16},{24,28},{28,24},{1,5},{5... | collective-permute-start | bytes 393224 | tf_op jit(solution)/shard_map/ppermute | solution.py:359
  68.7 11.2 %collective-permute-start.29 = (f32[256,128]{1,0:T(8,128)S(1)}, f32[256,128]{1,0:T(8,128)S(1)}, u32[]{:S(2)}, u32[]{:S(2)}) collective-permute-start(f32[256,128]{1,0:T(8,128)S(1)} %get-tuple-element.186), channel_id=1, source_target_pairs={{0,8},{4,12},{8,0},{12,4},{16,24},{20,28},{24,16},{28,20},{1,9},{5... | collective-permute-start | bytes 393224 | tf_op jit(solution)/shard_map/ppermute | solution.py:359
  69.7 10.3 %collective-permute-start.30 = (f32[256,128]{1,0:T(8,128)S(1)}, f32[256,128]{1,0:T(8,128)S(1)}, u32[]{:S(2)}, u32[]{:S(2)}) collective-permute-start(f32[256,128]{1,0:T(8,128)S(1)} %get-tuple-element.187), channel_id=1, source_target_pairs={{0,12},{4,8},{8,4},{12,0},{16,28},{20,24},{24,20},{28,16},{1,13},{... | collective-permute-start | bytes 393224 | tf_op jit(solution)/shard_map/ppermute | solution.py:359
  73.1 9.3 %collective-permute-start.25 = (f32[264,128]{1,0:T(8,128)S(1)}, f32[264,128]{1,0:T(8,128)S(1)}, u32[]{:S(2)}, u32[]{:S(2)}) collective-permute-start(f32[264,128]{1,0:T(8,128)S(1)} %get-tuple-element.170), channel_id=1, source_target_pairs={{0,4},{4,0},{8,12},{12,8},{16,20},{20,16},{24,28},{28,24},{1,5},{5... | collective-permute-start | bytes 405512 | tf_op jit(solution)/shard_map/ppermute | solution.py:359
  74.3 8.1 %collective-permute-start.26 = (f32[264,128]{1,0:T(8,128)S(1)}, f32[264,128]{1,0:T(8,128)S(1)}, u32[]{:S(2)}, u32[]{:S(2)}) collective-permute-start(f32[264,128]{1,0:T(8,128)S(1)} %get-tuple-element.171), channel_id=1, source_target_pairs={{0,8},{4,12},{8,0},{12,4},{16,24},{20,28},{24,16},{28,20},{1,9},{5... | collective-permute-start | bytes 405512 | tf_op jit(solution)/shard_map/ppermute | solution.py:359
  (11 other events, 69.8 us)
